TPU v7x, 32 devices: a whole 2x2x4 slice. The times are simulated.
32 devices in a mesh: node: 8 (over y, x, core), local: 4 (over z).
Axes of the slice: x: 2, y: 2, z: 4, core: 2. Of those that a mesh axis runs over, the one named last changes fastest.
Arguments:
- expert_ids: int32 [4096, 4], P(('node', 'local')), may hold values from 0 to 31, as said below
- gate_weights: bfloat16 [4096, 4], P(('node', 'local')), may hold values from 0.099609375 to 1
- tokens_in: bfloat16 [4096, 3584], P(('node', 'local')), may hold values from -6 to 6
- grad_out: bfloat16 [4096, 3584], P(('node', 'local')), may hold values from -6 to 6
- w_gate: bfloat16 [32, 3584, 1024], P(('node', 'local')), may hold values from -0.09375 to 0.09375
- w_up: bfloat16 [32, 3584, 1024], P(('node', 'local')), may hold values from -0.09375 to 0.09375
- w_down: bfloat16 [32, 1024, 3584], P(('node', 'local')), may hold values from -0.1875 to 0.1875
Outputs:
- grad_in: bfloat16 [4096, 3584], P(('node', 'local'))
Inputs may be any that keep to these rules, and one draw needn't show every extreme that they name: `expert_ids`: each token names 4 different experts, two in each of two different node groups; node group m holds experts 4 m to 4 m + 3. The tokens of one device pick every node group exactly 32 times. From the tokens of one device every expert gets at most 24 rows; in every node group one expert gets exactly 24 rows from every device, the others fewer, and every expert gets some rows.
All inputs are finite; a program needn't handle non-finite values.
Results may differ from a plain program's by a relative error of at most 0.0064.
Values may be sent and summed in bfloat16 or wider, within the bound.
No kernel may reach another device: no remote copies, remote signals or barrier semaphores. Data moves between devices by JAX's collectives and lax.ppermute only.
A program may use at most 128 MiB of HBM per device.

v0:
```python
import functools

import jax
import jax.numpy as jnp
from jax import lax
from jax.experimental import pallas as pl
from jax.experimental.pallas import tpu as pltpu
from jax.sharding import PartitionSpec as P

NEAR = [(0, 1), (1, 0), (2, 3), (3, 2)]
ACROSS = [(1, 2), (2, 1)]
OUTWARD = [(1, 0), (2, 3)]
INWARD = [(0, 1), (3, 2)]
OUTSIDE = [(1, 3), (2, 0)]

LANES = 128
WIDE = 512
VMEM = 60 * 1024 * 1024
PACE = 2000000000
WHOLE = (2, 3)
COSTS = {
    "route": 3, "dispatch0": 4, "dispatch1": 4, "dispatch2": 4, "dispatch3": 4,
    "experts0": 18, "experts1": 18, "experts2": 18, "experts3": 18,
    "combine0": 3, "combine1": 3, "combine2": 3, "combine3": 3,
}
FIRST = (((1,), (0,)), ((), ()))
SECOND = (((1,), (1,)), ((), ()))
ROWS = (((0,), (0,)), ((), ()))


def dot(left, right, dims=FIRST):
    return lax.dot_general(left, right, dims, preferred_element_type=jnp.float32)


def call(body, operands, after, outs, name, specs=None, **more):
    whole = pl.BlockSpec(memory_space=pltpu.VMEM)
    specs = specs or [whole] * len(operands)
    count = len(operands)

    def kernel(*refs):
        body(*refs[:count], *refs[count + len(after) :])

    return pl.pallas_call(
        kernel,
        in_specs=specs + [pl.BlockSpec(memory_space=pl.ANY)] * len(after),
        out_shape=outs,
        compiler_params=pltpu.CompilerParams(vmem_limit_bytes=VMEM),
        cost_estimate=pl.CostEstimate(
            flops=int(COSTS[name] * PACE), bytes_accessed=1000, transcendentals=0
        ),
        name=name,
        **more,
    )(*operands, *after)


def shape(*dims):
    return jax.ShapeDtypeStruct(dims, jnp.bfloat16)


def columns(width):
    return [(start, min(WIDE, width - start)) for start in range(0, width, WIDE)]


def route(expert_ids, gate_weights, tokens, grads, expert_count):
    count, width = tokens.shape
    top = expert_ids.shape[1]

    def body(ids_ref, weights_ref, tokens_ref, grads_ref, out_ref):
        ids = ids_ref[...]
        experts = lax.broadcasted_iota(jnp.int32, (expert_count, count), 0)
        named = [(ids[k : k + 1] == experts).astype(jnp.float32) for k in range(top)]
        onehot = functools.reduce(jnp.add, named).astype(jnp.bfloat16)
        first = lax.broadcasted_iota(jnp.int32, (count, count), 0)
        second = lax.broadcasted_iota(jnp.int32, (count, count), 1)
        before = dot(onehot, (first < second).astype(jnp.bfloat16))
        ranks = [jnp.sum(one * before, axis=0, keepdims=True) for one in named]
        pad = -3 * top % 8
        table = [ids.astype(jnp.float32)] + ranks + [weights_ref[...].astype(jnp.float32)]
        table = jnp.concatenate(table + [jnp.zeros((pad, count), jnp.float32)], axis=0)
        same = lax.broadcasted_iota(jnp.int32, (3 * top + pad, LANES), 0)
        same = same == lax.broadcasted_iota(jnp.int32, (3 * top + pad, LANES), 1)
        out_ref[:, :width] = tokens_ref[...]
        out_ref[:, width : 2 * width] = grads_ref[...]
        out_ref[:, 2 * width :] = dot(
            table.astype(jnp.bfloat16), same.astype(jnp.bfloat16), ROWS
        ).astype(jnp.bfloat16)

    operands = (expert_ids.T, gate_weights.T, tokens, grads)
    return call(body, operands, (), shape(count, 2 * width + LANES), "route")


def dispatch(step, sizes, top, place, chunk, after):
    nodes, local_count, slots = sizes
    count = chunk[0].shape[0]
    width = (chunk[0].shape[1] - LANES) // 2

    def body(place_ref, *refs):
        chunk_refs, (out_ref, picks_ref, xor_ref) = refs[:-3], refs[-3:]
        node, local = place_ref[0], place_ref[1]

        def tile(start, size):
            return functools.reduce(jnp.add, [c[:, start : start + size] for c in chunk_refs])

        first = lax.broadcasted_iota(jnp.int32, (count, count), 0)
        second = lax.broadcasted_iota(jnp.int32, (count, count), 1)
        table = dot(tile(2 * width, LANES), (first == second).astype(jnp.bfloat16), ROWS)
        slot = lax.broadcasted_iota(jnp.int32, (slots, count), 0).astype(jnp.float32)

        def choose(other):
            wanted = (other * local_count + local).astype(jnp.float32)
            pick = jnp.zeros((slots, count), jnp.float32)
            weigh = jnp.zeros((slots, count), jnp.float32)
            for k in range(top):
                hit = (table[k : k + 1] == wanted) & (table[top + k : top + k + 1] == slot)
                pick = jnp.where(hit, 1.0, pick)
                weigh = jnp.where(hit, table[2 * top + k : 2 * top + k + 1], weigh)
            return pick, weigh

        def stack(parts):
            return jnp.concatenate(parts, axis=0).astype(jnp.bfloat16)

        chosen = [choose(jnp.int32(j)) for j in range(nodes)]
        picks, weighed = stack([c[0] for c in chosen]), stack([c[1] for c in chosen])
        picks_ref[...] = picks
        xor_ref[...] = stack([choose(jnp.bitwise_xor(node, j))[0] for j in range(nodes)])
        for start, size in columns(width):
            taken = dot(picks, tile(start, size))
            out_ref[:, start : start + size] = taken.astype(jnp.bfloat16)
            taken = dot(weighed, tile(width + start, size))
            out_ref[:, width + start : width + start + size] = taken.astype(jnp.bfloat16)

    return call(
        body,
        (place, *chunk),
        after,
        [shape(nodes * slots, 2 * width)] + [shape(nodes * slots, count)] * 2,
        f"dispatch{step}",
        [pl.BlockSpec(memory_space=pltpu.SMEM)]
        + [pl.BlockSpec(memory_space=pltpu.VMEM)] * len(chunk),
    )


def experts(step, blocks, nodes, place, rows, w_gate, w_up, w_down, after):
    count, wide = rows.shape
    slots, width = count // nodes, wide // 2
    hidden = w_gate.shape[2]
    step_width = 512

    def body(place_ref, rows_ref, gate_ref, up_ref, down_ref, *refs):
        outs, sum_ref = refs[:blocks], refs[blocks]
        step = pl.program_id(0)

        @pl.when(step == 0)
        def _():
            sum_ref[...] = jnp.zeros_like(sum_ref)

        pre_gate = dot(rows_ref[:, :width], gate_ref[0])
        pre_up = dot(rows_ref[:, :width], up_ref[0])
        grad_hidden = dot(rows_ref[:, width:], down_ref[0], SECOND)
        sigmoid_gate = 1.0 / (1.0 + jnp.exp(-pre_gate))
        grad_gate = (
            grad_hidden * pre_up * sigmoid_gate * (1.0 + pre_gate * (1.0 - sigmoid_gate))
        ).astype(jnp.bfloat16)
        grad_up = (grad_hidden * pre_gate * sigmoid_gate).astype(jnp.bfloat16)
        for start, size in columns(width):
            part = dot(grad_gate, gate_ref[0, start : start + size, :], SECOND)
            part = part + dot(grad_up, up_ref[0, start : start + size, :], SECOND)
            sum_ref[:, start : start + size] += part

        @pl.when(step == pl.num_programs(0) - 1)
        def _():
            if blocks == 1:
                outs[0][...] = sum_ref[...].astype(jnp.bfloat16)
            else:
                for j in range(blocks):
                    start = pl.multiple_of(jnp.bitwise_xor(place_ref[0], j) * slots, 8)
                    outs[j][...] = sum_ref[pl.ds(start, slots), :].astype(jnp.bfloat16)

    across = pl.BlockSpec((1, width, step_width), lambda f: (0, 0, f))
    return call(
        body,
        (place, rows, w_gate, w_up, w_down),
        after,
        [shape(count // blocks, width)] * blocks,
        f"experts{step}",
        [
            pl.BlockSpec(memory_space=pltpu.SMEM),
            pl.BlockSpec((count, wide), lambda f: (0, 0)),
            across,
            across,
            pl.BlockSpec((1, step_width, width), lambda f: (0, f, 0)),
        ],
        grid=(hidden // step_width,),
        out_specs=[pl.BlockSpec((count // blocks, width), lambda f: (0, 0))] * blocks,
        scratch_shapes=[pltpu.VMEM((count, width), jnp.float32)],
    )


def combine(step, blocks, picks, added, after):
    nodes = len(blocks)
    width = blocks[0].shape[1]

    def body(*refs):
        block_refs, picks_ref = refs[:nodes], refs[nodes]
        added_refs, out_ref = refs[nodes + 1 : -1], refs[-1]
        picks = picks_ref[...]
        for start, size in columns(width):
            rows = [b[:, start : start + size].astype(jnp.float32) for b in block_refs]
            total = dot(picks, jnp.concatenate(rows, axis=0).astype(jnp.bfloat16), ROWS)
            for other in added_refs:
                total = total + other[:, start : start + size].astype(jnp.float32)
            out_ref[:, start : start + size] = total.astype(jnp.bfloat16)

    out = shape(picks.shape[1], width)
    return call(body, (*blocks, picks, *added), after, out, f"combine{step}")


def along(rows, pairs):
    return lax.ppermute(rows, "local", pairs)


def give_back(blocks):
    count = len(blocks)
    return [blocks[0]] + [
        lax.ppermute(blocks[j], "node", [(i, i ^ j) for i in range(count)])
        for j in range(1, count)
    ]


def per_device(expert_ids, gate_weights, tokens_in, grad_out, w_gate, w_up, w_down):
    token_count, width = tokens_in.shape
    top = expert_ids.shape[1]
    node_count = lax.axis_size("node")
    local_count = lax.axis_size("local")
    visits = 2 * token_count // node_count
    slots = -(-(3 * visits // 4) // 8) * 8
    sizes = (node_count, local_count, slots)
    place = jnp.stack([lax.axis_index("node"), lax.axis_index("local")]).astype(jnp.int32)

    def over_nodes(rows):
        cut = rows.reshape(node_count, slots, -1)
        return lax.all_to_all(cut, "node", 0, 0, tiled=True).reshape(rows.shape)

    experts_in_all = node_count * local_count
    routed = route(expert_ids, gate_weights, tokens_in, grad_out, experts_in_all)
    near = along(routed, NEAR)
    across = along(routed, ACROSS)
    far = along(near, ACROSS)
    chunks = (
        (routed,),
        (near,),
        (across, along(across, OUTWARD)),
        (far, along(far, OUTWARD)),
    )
    last = ()
    sent, picks, xors, back, sums = [[None] * 4 for _ in range(5)]

    def send(k):
        nonlocal last
        rows, picks[k], xors[k] = dispatch(k, sizes, top, place, chunks[k], last)
        last = (picks[k],)
        sent[k] = over_nodes(rows)

    def work(k):
        nonlocal last
        count = 1 if k in WHOLE else node_count
        out = experts(k, count, node_count, place, sent[k], w_gate, w_up, w_down, last)
        last = (out[0],)
        back[k] = [over_nodes(out[0])] if count == 1 else give_back(out)

    def gather(k, *added):
        nonlocal last
        chosen = picks[k] if k in WHOLE else xors[k]
        sums[k] = combine(k, back[k], chosen, added, last)
        last = (sums[k],)
        return sums[k]

    def late(array):
        nonlocal last
        last = last + (array,)

    send(0)
    send(1)
    work(0)
    send(2)
    gather(0)
    work(1)
    send(3)
    near = along(gather(1), NEAR)
    work(2)
    late(near)
    work(3)
    across = along(gather(2), INWARD)
    far = gather(3)
    across = along(sums[2] + across, ACROSS)
    outside = along(far + along(far, INWARD), OUTSIDE)
    total = sums[0].astype(jnp.float32)
    for part in (near, across, outside):
        total = total + part.astype(jnp.float32)
    return total.astype(jnp.bfloat16)


def solution(mesh):
    flat = P(("node", "local"), None)
    deep = P(("node", "local"), None, None)
    return jax.shard_map(
        per_device,
        mesh=mesh,
        in_specs=(flat, flat, flat, flat, deep, deep, deep),
        out_specs=flat,
        check_vma=False,
    )
```

profile of v0, /device:TPU:0, one launch (start us, length us, event | category | flops | bytes accessed | tf_op | source)
XLA Modules:
  0.0 316.5 jit_solution(2021204144347177185)
XLA Ops:
  0.0 3.1 route.1.refs_1_
  3.1 3.0 collective-permute-start
  8.7 4.1 %dispatch0.1 = (bf16[192,7168]{1,0:T(8,128)(2,1)}, bf16[192,128]{1,0:T(8,128)(2,1)}, bf16[192,128]{1,0:T(8,128)(2,1)}) custom-call(s32[2]{0:T(128)} %pad_add_fusion.refs_0_, bf16[128,7296]{1,0:T(8,128)(2,1)} %route.1.refs_1_), custom_call_target="tpu_custom_call" | custom-call | flops 8000000000 | bytes 1000 | tf_op jit(solution)/shard_map/dispatch0/pallas_call | solution.py:43
  12.8 3.7 %all-to-all-start = ((bf16[8,24,7168]{2,1,0:T(8,128)(2,1)}), bf16[8,24,7168]{2,1,0:T(8,128)(2,1)S(1)}, u32[]{:S(2)}, u32[]{:S(2)}) async-start(bf16[8,24,7168]{2,1,0:T(8,128)(2,1)} %bitcast.19), calls=%async_computation | async-start | bytes 5505024 | tf_op jit(solution)/shard_map/all_to_all | solution.py:242
  17.8 29.3 %collective-permute-done.refs_1_ = bf16[128,7296]{1,0:T(8,128)(2,1)} collective-permute-done((bf16[128,7296]{1,0:T(8,128)(2,1)}, bf16[128,7296]{1,0:T(8,128)(2,1)}, u32[]{:S(2)}, u32[]{:S(2)}) %collective-permute-start) | collective-permute-done | bytes 1867808 | tf_op jit(solution)/shard_map/ppermute | solution.py:219
  49.1 4.1 %dispatch1.1 = (bf16[192,7168]{1,0:T(8,128)(2,1)}, bf16[192,128]{1,0:T(8,128)(2,1)}, bf16[192,128]{1,0:T(8,128)(2,1)}) custom-call(s32[2]{0:T(128)} %pad_add_fusion.refs_0_, bf16[128,7296]{1,0:T(8,128)(2,1)} %collective-permute-done.refs_1_, bf16[192,128]{1,0:T(8,128)(2,1)} %get-tuple-element.32.refs_2_), custom_call_target="tpu_custom_call" | custom-call | flops 8000000000 | bytes 1000 | tf_op jit(solution)/shard_map/dispatch1/pallas_call | solution.py:43
  54.7 3.9 %all-to-all-start.1 = ((bf16[8,24,7168]{2,1,0:T(8,128)(2,1)}), bf16[8,24,7168]{2,1,0:T(8,128)(2,1)S(1)}, u32[]{:S(2)}, u32[]{:S(2)}) async-start(bf16[8,24,7168]{2,1,0:T(8,128)(2,1)} %bitcast.17), calls=%async_computation.1 | async-start | bytes 5505024 | tf_op jit(solution)/shard_map/all_to_all | solution.py:242
  58.6 17.9 %experts0.1 = (bf16[24,3584]{1,0:T(8,128)(2,1)}, bf16[24,3584]{1,0:T(8,128)(2,1)}, bf16[24,3584]{1,0:T(8,128)(2,1)}, bf16[24,3584]{1,0:T(8,128)(2,1)}, bf16[24,3...) custom-call(s32[2]{0:T(128)} %pad_add_fusion.refs_0_, ...), custom_call_target="tpu_custom_call" | custom-call | flops 35999997952 | bytes 1000 | tf_op jit(solution)/shard_map/experts0/pallas_call | solution.py:43
  80.4 15.2 %collective-permute-done.2.refs_2_ = bf16[24,3584]{1,0:T(8,128)(2,1)S(1)} collective-permute-done((bf16[24,3584]{1,0:T(8,128)(2,1)}, bf16[24,3584]{1,0:T(8,128)(2,1)S(1)}, u32[]{:S(2)}, u32[]{:S(2)}) %collective-permute-start.2) | collective-permute-done | bytes 172064 | tf_op jit(solution)/shard_map/ppermute | solution.py:225
  95.8 2.5 collective-permute-done.3.refs_3_
  101.2 4.7 %dispatch2.1 = (bf16[192,7168]{1,0:T(8,128)(2,1)}, bf16[192,128]{1,0:T(8,128)(2,1)}, bf16[192,128]{1,0:T(8,128)(2,1)}) custom-call(s32[2]{0:T(128)} %pad_add_fusion.refs_0_, bf16[128,7296]{1,0:T(8,128)(2,1)} %collective-permute-done.8.refs_1_, bf16[128,7296]{1,0:T(8,128)(2,1)} %collective-permute-done.9.refs_2_, ...), custom_call_target="tpu_custom_call" | custom-call | flops 8000000000 | bytes 1000 | tf_op jit(solution)/shard_map/dispatch2/pallas_call | solution.py:43
  107.2 2.5 collective-permute-done.7.refs_7_
  110.4 2.8 combine0.1.refs_5_
  114.7 4.6 %all-to-all-start.2 = ((bf16[8,24,7168]{2,1,0:T(8,128)(2,1)}), bf16[8,24,7168]{2,1,0:T(8,128)(2,1)}, u32[]{:S(2)}, u32[]{:S(2)}) async-start(bf16[8,24,7168]{2,1,0:T(8,128)(2,1)} %bitcast.8), calls=%async_computation.2 | async-start | bytes 5505024 | tf_op jit(solution)/shard_map/all_to_all | solution.py:242
  119.3 17.9 %experts1.1 = (bf16[24,3584]{1,0:T(8,128)(2,1)}, bf16[24,3584]{1,0:T(8,128)(2,1)}, bf16[24,3584]{1,0:T(8,128)(2,1)}, bf16[24,3584]{1,0:T(8,128)(2,1)}, bf16[24,3...) custom-call(s32[2]{0:T(128)} %pad_add_fusion.refs_0_, ...), custom_call_target="tpu_custom_call" | custom-call | flops 35999997952 | bytes 1000 | tf_op jit(solution)/shard_map/experts1/pallas_call | solution.py:43
  141.0 15.0 %collective-permute-done.11.refs_2_ = bf16[24,3584]{1,0:T(8,128)(2,1)S(1)} collective-permute-done((bf16[24,3584]{1,0:T(8,128)(2,1)}, bf16[24,3584]{1,0:T(8,128)(2,1)S(1)}, u32[]{:S(2)}, u32[]{:S(2)}) %collective-permute-start.11) | collective-permute-done | bytes 172064 | tf_op jit(solution)/shard_map/ppermute | solution.py:225
  158.2 4.7 %dispatch3.1 = (bf16[192,7168]{1,0:T(8,128)(2,1)}, bf16[192,128]{1,0:T(8,128)(2,1)}, bf16[192,128]{1,0:T(8,128)(2,1)}) custom-call(s32[2]{0:T(128)} %pad_add_fusion.refs_0_, bf16[128,7296]{1,0:T(8,128)(2,1)} %collective-permute-done.17.refs_1_, bf16[128,7296]{1,0:T(8,128)(2,1)} %collective-permute-done.18.refs_2_, ...), custom_call_target="tpu_custom_call" | custom-call | flops 8000000000 | bytes 1000 | tf_op jit(solution)/shard_map/dispatch3/pallas_call | solution.py:43
  164.4 2.5 collective-permute-done.16.refs_7_
  167.6 2.8 combine1.1.refs_5_
  170.4 8.9 %collective-permute-start.19 = (bf16[128,3584]{1,0:T(8,128)(2,1)}, bf16[128,3584]{1,0:T(8,128)(2,1)}, u32[]{:S(2)}, u32[]{:S(2)}) collective-permute-start(bf16[128,3584]{1,0:T(8,128)(2,1)} %combine1.1.refs_5_), channel_id=1, source_target_pairs={{0,1},{1,0},{2,3},{3,2},{4,5},{5,4},{6,7},{7,6},{8,9},{9,8},{10,11... | collective-permute-start | bytes 2752520 | tf_op jit(solution)/shard_map/ppermute | solution.py:219
  179.2 3.6 %all-to-all-start.4 = ((bf16[8,24,7168]{2,1,0:T(8,128)(2,1)}), bf16[8,24,7168]{2,1,0:T(8,128)(2,1)S(1)}, u32[]{:S(2)}, u32[]{:S(2)}) async-start(bf16[8,24,7168]{2,1,0:T(8,128)(2,1)} %bitcast.12), calls=%async_computation.4 | async-start | bytes 5505024 | tf_op jit(solution)/shard_map/all_to_all | solution.py:242
  182.8 17.9 %experts2.1.refs_5_ = bf16[192,3584]{1,0:T(8,128)(2,1)} custom-call(s32[2]{0:T(128)} %pad_add_fusion.refs_0_, bf16[192,7168]{1,0:T(8,128)(2,1)} %bitcast.9.refs_1_, bf16[1,3584,1024]{2,1,0:T(8,128)(2,1)} %refs_2_.9, bf16[1,3584,1024]{2,1,0:T(8,128)(2,1)} %refs_3_.9, bf16[1,1024,3584]{2,1,0:T(8,128)(2,1)} %refs_4_.7, bf16[128,3584]{1,0:T(8,128)(2,1)} %combine1.1.refs_5_), custom_call_target="tpu_custom_call" | custom-call | flops 35999997952 | bytes 1000 | tf_op jit(solution)/shard_map/experts2/pallas_call | solution.py:43
  200.7 15.7 %all-to-all-done.4 = bf16[8,24,7168]{2,1,0:T(8,128)(2,1)S(1)} async-done(((bf16[8,24,7168]{2,1,0:T(8,128)(2,1)}), bf16[8,24,7168]{2,1,0:T(8,128)(2,1)S(1)}, u32[]{:S(2)}, u32[]{:S(2)}) %all-to-all-start.4) | async-done | bytes 2752544 | tf_op jit(solution)/shard_map/all_to_all | solution.py:242
  216.4 4.5 %all-to-all-start.3 = ((bf16[8,24,3584]{2,1,0:T(8,128)(2,1)}), bf16[8,24,3584]{2,1,0:T(8,128)(2,1)}, u32[]{:S(2)}, u32[]{:S(2)}) async-start(bf16[8,24,3584]{2,1,0:T(8,128)(2,1)} %bitcast.22), calls=%async_computation.3 | async-start | bytes 2752512 | tf_op jit(solution)/shard_map/all_to_all | solution.py:242
  221.0 17.9 %experts3.1.refs_2_ = bf16[192,3584]{1,0:T(8,128)(2,1)} custom-call(s32[2]{0:T(128)} %pad_add_fusion.refs_0_, bf16[192,7168]{1,0:T(8,128)(2,1)} %bitcast.20, bf16[1,3584,1024]{2,1,0:T(8,128)(2,1)} %refs_2_.9, bf16[1,3584,1024]{2,1,0:T(8,128)(2,1)} %refs_3_.9, bf16[1,1024,3584]{2,1,0:T(8,128)(2,1)} %refs_4_.7, bf16[192,3584]{1,0:T(8,128)(2,1)} %experts2.1.refs_5_, ...), custom_call_target="tpu_custom_call" | custom-call | flops 35999997952 | bytes 1000 | tf_op jit(solution)/shard_map/experts3/pallas_call | solution.py:43
  239.7 3.6 %all-to-all-start.5 = ((bf16[8,24,3584]{2,1,0:T(8,128)(2,1)}), bf16[8,24,3584]{2,1,0:T(8,128)(2,1)S(1)}, u32[]{:S(2)}, u32[]{:S(2)}) async-start(bf16[8,24,3584]{2,1,0:T(8,128)(2,1)} %bitcast.21), calls=%async_computation.5 | async-start | bytes 2752512 | tf_op jit(solution)/shard_map/all_to_all | solution.py:242
  243.2 2.7 combine2.1.refs_2_
  248.0 14.1 %all-to-all-done.5 = bf16[8,24,3584]{2,1,0:T(8,128)(2,1)S(1)} async-done(((bf16[8,24,3584]{2,1,0:T(8,128)(2,1)}), bf16[8,24,3584]{2,1,0:T(8,128)(2,1)S(1)}, u32[]{:S(2)}, u32[]{:S(2)}) %all-to-all-start.5) | async-done | bytes 1376288 | tf_op jit(solution)/shard_map/all_to_all | solution.py:242
  263.2 2.8 combine3.1
  270.0 18.0 %collective-permute-done.22 = bf16[128,3584]{1,0:T(8,128)(2,1)S(1)} collective-permute-done((bf16[128,3584]{1,0:T(8,128)(2,1)}, bf16[128,3584]{1,0:T(8,128)(2,1)S(1)}, u32[]{:S(2)}, u32[]{:S(2)}) %collective-permute-start.22) | collective-permute-done | bytes 917536 | tf_op jit(solution)/shard_map/ppermute | solution.py:219
  289.5 24.4 %collective-permute-done.23 = bf16[128,3584]{1,0:T(8,128)(2,1)S(1)} collective-permute-done((bf16[128,3584]{1,0:T(8,128)(2,1)S(1)}, bf16[128,3584]{1,0:T(8,128)(2,1)S(1)}, u32[]{:S(2)}, u32[]{:S(2)}) %collective-permute-start.23) | collective-permute-done | bytes 917536 | tf_op jit(solution)/shard_map/ppermute | solution.py:219
  313.9 2.6 add_convert_fusion
  (87 shorter events, 35.2 us)
Async XLA Ops:
  3.1 44.1 %collective-permute-start = (bf16[128,7296]{1,0:T(8,128)(2,1)}, bf16[128,7296]{1,0:T(8,128)(2,1)}, u32[]{:S(2)}, u32[]{:S(2)}) collective-permute-start(bf16[128,7296]{1,0:T(8,128)(2,1)} %route.1.refs_1_), channel_id=1, source_target_pairs={{0,1},{1,0},{2,3},{3,2},{4,5},{5,4},{6,7},{7,6},{8,9},{9,8},{10,11... | collective-permute-start | bytes 5603336 | tf_op jit(solution)/shard_map/ppermute | solution.py:219
  6.2 10.4 %collective-permute-start.8 = (bf16[128,7296]{1,0:T(8,128)(2,1)}, bf16[128,7296]{1,0:T(8,128)(2,1)}, u32[]{:S(2)}, u32[]{:S(2)}) collective-permute-start(bf16[128,7296]{1,0:T(8,128)(2,1)} %route.1.refs_1_), channel_id=1, source_target_pairs={{1,2},{2,1},{5,6},{6,5},{9,10},{10,9},{13,14},{14,13},{17,18},{18,... | collective-permute-start | bytes 5603336 | tf_op jit(solution)/shard_map/ppermute | solution.py:219
  12.8 40.4 %all-to-all-start = ((bf16[8,24,7168]{2,1,0:T(8,128)(2,1)}), bf16[8,24,7168]{2,1,0:T(8,128)(2,1)S(1)}, u32[]{:S(2)}, u32[]{:S(2)}) async-start(bf16[8,24,7168]{2,1,0:T(8,128)(2,1)} %bitcast.19), calls=%async_computation | async-start | bytes 5505024 | tf_op jit(solution)/shard_map/all_to_all | solution.py:242
  16.5 83.3 %collective-permute-start.9 = (bf16[128,7296]{1,0:T(8,128)(2,1)}, bf16[128,7296]{1,0:T(8,128)(2,1)}, u32[]{:S(2)}, u32[]{:S(2)}) collective-permute-start(bf16[128,7296]{1,0:T(8,128)(2,1)} %collective-permute-done.8.refs_1_), channel_id=1, source_target_pairs={{1,0},{2,3},{5,4},{6,7},{9,8},{10,11},{13,12},{14,15},{17,16},{18,... | collective-permute-start | bytes 5603336 | tf_op jit(solution)/shard_map/ppermute | solution.py:219
  47.2 58.7 %collective-permute-start.17 = (bf16[128,7296]{1,0:T(8,128)(2,1)}, bf16[128,7296]{1,0:T(8,128)(2,1)}, u32[]{:S(2)}, u32[]{:S(2)}) collective-permute-start(bf16[128,7296]{1,0:T(8,128)(2,1)} %collective-permute-done.refs_1_), channel_id=1, source_target_pairs={{1,2},{2,1},{5,6},{6,5},{9,10},{10,9},{13,14},{14,13},{17,18},{18,... | collective-permute-start | bytes 5603336 | tf_op jit(solution)/shard_map/ppermute | solution.py:219
  54.7 58.4 %all-to-all-start.1 = ((bf16[8,24,7168]{2,1,0:T(8,128)(2,1)}), bf16[8,24,7168]{2,1,0:T(8,128)(2,1)S(1)}, u32[]{:S(2)}, u32[]{:S(2)}) async-start(bf16[8,24,7168]{2,1,0:T(8,128)(2,1)} %bitcast.17), calls=%async_computation.1 | async-start | bytes 5505024 | tf_op jit(solution)/shard_map/all_to_all | solution.py:242
  76.5 2.2 collective-permute-start.1
  77.0 18.6 %collective-permute-start.2 = (bf16[24,3584]{1,0:T(8,128)(2,1)}, bf16[24,3584]{1,0:T(8,128)(2,1)S(1)}, u32[]{:S(2)}, u32[]{:S(2)}) collective-permute-start(bf16[24,3584]{1,0:T(8,128)(2,1)} %get-tuple-element.36), channel_id=1, source_target_pairs={{0,8},{4,12},{8,0},{12,4},{16,24},{20,28},{24,16},{28,20},{1,9},{5... | collective-permute-start | bytes 516104 | tf_op jit(solution)/shard_map/ppermute | solution.py:225
  78.7 19.6 %collective-permute-start.3 = (bf16[24,3584]{1,0:T(8,128)(2,1)}, bf16[24,3584]{1,0:T(8,128)(2,1)S(1)}, u32[]{:S(2)}, u32[]{:S(2)}) collective-permute-start(bf16[24,3584]{1,0:T(8,128)(2,1)} %get-tuple-element.37), channel_id=1, source_target_pairs={{0,12},{4,8},{8,4},{12,0},{16,28},{20,24},{24,20},{28,16},{1,13},{... | collective-permute-start | bytes 516104 | tf_op jit(solution)/shard_map/ppermute | solution.py:225
  78.7 27.1 %copy-start.7 = (bf16[24,3584]{1,0:T(8,128)(2,1)}, bf16[24,3584]{1,0:T(8,128)(2,1)S(1)}, u32[]{:S(2)}) copy-start(bf16[24,3584]{1,0:T(8,128)(2,1)S(1)} %collective-permute-done.1.refs_1_) | copy-start | bytes 516100
  78.7 28.5 %collective-permute-start.4 = (bf16[24,3584]{1,0:T(8,128)(2,1)}, bf16[24,3584]{1,0:T(8,128)(2,1)S(1)}, u32[]{:S(2)}, u32[]{:S(2)}) collective-permute-start(bf16[24,3584]{1,0:T(8,128)(2,1)} %get-tuple-element.38), channel_id=1, source_target_pairs={{0,16},{4,20},{8,24},{12,28},{16,0},{20,4},{24,8},{28,12},{1,17},{... | collective-permute-start | bytes 516104 | tf_op jit(solution)/shard_map/ppermute | solution.py:225
  95.6 11.6 %collective-permute-start.5 = (bf16[24,3584]{1,0:T(8,128)(2,1)}, bf16[24,3584]{1,0:T(8,128)(2,1)S(1)}, u32[]{:S(2)}, u32[]{:S(2)}) collective-permute-start(bf16[24,3584]{1,0:T(8,128)(2,1)} %get-tuple-element.39), channel_id=1, source_target_pairs={{0,20},{4,16},{8,28},{12,24},{16,4},{20,0},{24,12},{28,8},{1,21},{... | collective-permute-start | bytes 516104 | tf_op jit(solution)/shard_map/ppermute | solution.py:225
  98.3 8.9 %collective-permute-start.6 = (bf16[24,3584]{1,0:T(8,128)(2,1)}, bf16[24,3584]{1,0:T(8,128)(2,1)S(1)}, u32[]{:S(2)}, u32[]{:S(2)}) collective-permute-start(bf16[24,3584]{1,0:T(8,128)(2,1)} %get-tuple-element.40), channel_id=1, source_target_pairs={{0,24},{4,28},{8,16},{12,20},{16,8},{20,12},{24,0},{28,4},{1,25},{... | collective-permute-start | bytes 516104 | tf_op jit(solution)/shard_map/ppermute | solution.py:225
  99.8 9.9 %collective-permute-start.7 = (bf16[24,3584]{1,0:T(8,128)(2,1)}, bf16[24,3584]{1,0:T(8,128)(2,1)S(1)}, u32[]{:S(2)}, u32[]{:S(2)}) collective-permute-start(bf16[24,3584]{1,0:T(8,128)(2,1)} %get-tuple-element.41), channel_id=1, source_target_pairs={{0,28},{4,24},{8,20},{12,16},{16,12},{20,8},{24,4},{28,0},{1,29},{... | collective-permute-start | bytes 516104 | tf_op jit(solution)/shard_map/ppermute | solution.py:225
  105.9 51.6 %collective-permute-start.18 = (bf16[128,7296]{1,0:T(8,128)(2,1)}, bf16[128,7296]{1,0:T(8,128)(2,1)}, u32[]{:S(2)}, u32[]{:S(2)}) collective-permute-start(bf16[128,7296]{1,0:T(8,128)(2,1)} %collective-permute-done.17.refs_1_), channel_id=1, source_target_pairs={{1,0},{2,3},{5,4},{6,7},{9,8},{10,11},{13,12},{14,15},{17,16},{18,... | collective-permute-start | bytes 5603336 | tf_op jit(solution)/shard_map/ppermute | solution.py:219
  114.7 64.5 %all-to-all-start.2 = ((bf16[8,24,7168]{2,1,0:T(8,128)(2,1)}), bf16[8,24,7168]{2,1,0:T(8,128)(2,1)}, u32[]{:S(2)}, u32[]{:S(2)}) async-start(bf16[8,24,7168]{2,1,0:T(8,128)(2,1)} %bitcast.8), calls=%async_computation.2 | async-start | bytes 5505024 | tf_op jit(solution)/shard_map/all_to_all | solution.py:242
  137.3 3.6 %collective-permute-start.10 = (bf16[24,3584]{1,0:T(8,128)(2,1)}, bf16[24,3584]{1,0:T(8,128)(2,1)S(1)}, u32[]{:S(2)}, u32[]{:S(2)}) collective-permute-start(bf16[24,3584]{1,0:T(8,128)(2,1)} %get-tuple-element.46), channel_id=1, source_target_pairs={{0,4},{4,0},{8,12},{12,8},{16,20},{20,16},{24,28},{28,24},{1,5},{5... | collective-permute-start | bytes 516104 | tf_op jit(solution)/shard_map/ppermute | solution.py:225
  137.5 18.5 %collective-permute-start.11 = (bf16[24,3584]{1,0:T(8,128)(2,1)}, bf16[24,3584]{1,0:T(8,128)(2,1)S(1)}, u32[]{:S(2)}, u32[]{:S(2)}) collective-permute-start(bf16[24,3584]{1,0:T(8,128)(2,1)} %get-tuple-element.47), channel_id=1, source_target_pairs={{0,8},{4,12},{8,0},{12,4},{16,24},{20,28},{24,16},{28,20},{1,9},{5... | collective-permute-start | bytes 516104 | tf_op jit(solution)/shard_map/ppermute | solution.py:225
  139.1 23.8 %collective-permute-start.12 = (bf16[24,3584]{1,0:T(8,128)(2,1)}, bf16[24,3584]{1,0:T(8,128)(2,1)S(1)}, u32[]{:S(2)}, u32[]{:S(2)}) collective-permute-start(bf16[24,3584]{1,0:T(8,128)(2,1)} %get-tuple-element.48), channel_id=1, source_target_pairs={{0,12},{4,8},{8,4},{12,0},{16,28},{20,24},{24,20},{28,16},{1,13},{... | collective-permute-start | bytes 516104 | tf_op jit(solution)/shard_map/ppermute | solution.py:225
  139.2 23.8 %collective-permute-start.13 = (bf16[24,3584]{1,0:T(8,128)(2,1)}, bf16[24,3584]{1,0:T(8,128)(2,1)S(1)}, u32[]{:S(2)}, u32[]{:S(2)}) collective-permute-start(bf16[24,3584]{1,0:T(8,128)(2,1)} %get-tuple-element.49), channel_id=1, source_target_pairs={{0,16},{4,20},{8,24},{12,28},{16,0},{20,4},{24,8},{28,12},{1,17},{... | collective-permute-start | bytes 516104 | tf_op jit(solution)/shard_map/ppermute | solution.py:225
  140.9 22.1 %collective-permute-start.14 = (bf16[24,3584]{1,0:T(8,128)(2,1)}, bf16[24,3584]{1,0:T(8,128)(2,1)S(1)}, u32[]{:S(2)}, u32[]{:S(2)}) collective-permute-start(bf16[24,3584]{1,0:T(8,128)(2,1)} %get-tuple-element.50), channel_id=1, source_target_pairs={{0,20},{4,16},{8,28},{12,24},{16,4},{20,0},{24,12},{28,8},{1,21},{... | collective-permute-start | bytes 516104 | tf_op jit(solution)/shard_map/ppermute | solution.py:225
  156.0 8.4 %collective-permute-start.15 = (bf16[24,3584]{1,0:T(8,128)(2,1)}, bf16[24,3584]{1,0:T(8,128)(2,1)S(1)}, u32[]{:S(2)}, u32[]{:S(2)}) collective-permute-start(bf16[24,3584]{1,0:T(8,128)(2,1)} %get-tuple-element.51), channel_id=1, source_target_pairs={{0,24},{4,28},{8,16},{12,20},{16,8},{20,12},{24,0},{28,4},{1,25},{... | collective-permute-start | bytes 516104 | tf_op jit(solution)/shard_map/ppermute | solution.py:225
  157.5 9.4 %collective-permute-start.16 = (bf16[24,3584]{1,0:T(8,128)(2,1)}, bf16[24,3584]{1,0:T(8,128)(2,1)S(1)}, u32[]{:S(2)}, u32[]{:S(2)}) collective-permute-start(bf16[24,3584]{1,0:T(8,128)(2,1)} %get-tuple-element.52), channel_id=1, source_target_pairs={{0,28},{4,24},{8,20},{12,16},{16,12},{20,8},{24,4},{28,0},{1,29},{... | collective-permute-start | bytes 516104 | tf_op jit(solution)/shard_map/ppermute | solution.py:225
  170.4 50.6 %collective-permute-start.19 = (bf16[128,3584]{1,0:T(8,128)(2,1)}, bf16[128,3584]{1,0:T(8,128)(2,1)}, u32[]{:S(2)}, u32[]{:S(2)}) collective-permute-start(bf16[128,3584]{1,0:T(8,128)(2,1)} %combine1.1.refs_5_), channel_id=1, source_target_pairs={{0,1},{1,0},{2,3},{3,2},{4,5},{5,4},{6,7},{7,6},{8,9},{9,8},{10,11... | collective-permute-start | bytes 2752520 | tf_op jit(solution)/shard_map/ppermute | solution.py:219
  179.2 37.2 %all-to-all-start.4 = ((bf16[8,24,7168]{2,1,0:T(8,128)(2,1)}), bf16[8,24,7168]{2,1,0:T(8,128)(2,1)S(1)}, u32[]{:S(2)}, u32[]{:S(2)}) async-start(bf16[8,24,7168]{2,1,0:T(8,128)(2,1)} %bitcast.12), calls=%async_computation.4 | async-start | bytes 5505024 | tf_op jit(solution)/shard_map/all_to_all | solution.py:242
  216.4 23.2 %all-to-all-start.3 = ((bf16[8,24,3584]{2,1,0:T(8,128)(2,1)}), bf16[8,24,3584]{2,1,0:T(8,128)(2,1)}, u32[]{:S(2)}, u32[]{:S(2)}) async-start(bf16[8,24,3584]{2,1,0:T(8,128)(2,1)} %bitcast.22), calls=%async_computation.3 | async-start | bytes 2752512 | tf_op jit(solution)/shard_map/all_to_all | solution.py:242
  239.7 22.4 %all-to-all-start.5 = ((bf16[8,24,3584]{2,1,0:T(8,128)(2,1)}), bf16[8,24,3584]{2,1,0:T(8,128)(2,1)S(1)}, u32[]{:S(2)}, u32[]{:S(2)}) async-start(bf16[8,24,3584]{2,1,0:T(8,128)(2,1)} %bitcast.21), calls=%async_computation.5 | async-start | bytes 2752512 | tf_op jit(solution)/shard_map/all_to_all | solution.py:242
  245.9 22.9 %collective-permute-start.20 = (bf16[128,3584]{1,0:T(8,128)(2,1)}, bf16[128,3584]{1,0:T(8,128)(2,1)S(1)}, u32[]{:S(2)}, u32[]{:S(2)}) collective-permute-start(bf16[128,3584]{1,0:T(8,128)(2,1)} %combine2.1.refs_2_), channel_id=1, source_target_pairs={{0,1},{3,2},{4,5},{7,6},{8,9},{11,10},{12,13},{15,14},{16,17},{19,... | collective-permute-start | bytes 2752520 | tf_op jit(solution)/shard_map/ppermute | solution.py:219
  266.0 22.0 %collective-permute-start.22 = (bf16[128,3584]{1,0:T(8,128)(2,1)}, bf16[128,3584]{1,0:T(8,128)(2,1)S(1)}, u32[]{:S(2)}, u32[]{:S(2)}) collective-permute-start(bf16[128,3584]{1,0:T(8,128)(2,1)} %combine3.1), channel_id=1, source_target_pairs={{0,1},{3,2},{4,5},{7,6},{8,9},{11,10},{12,13},{15,14},{16,17},{19,... | collective-permute-start | bytes 2752520 | tf_op jit(solution)/shard_map/ppermute | solution.py:219
  269.1 44.8 %copy-start.4 = (bf16[128,3584]{1,0:T(8,128)(2,1)S(1)}, bf16[128,3584]{1,0:T(8,128)(2,1)}, u32[]{:S(2)}) copy-start(bf16[128,3584]{1,0:T(8,128)(2,1)} %combine0.1.refs_5_) | copy-start | bytes 2752516
  269.1 20.4 %collective-permute-start.21 = (bf16[128,3584]{1,0:T(8,128)(2,1)S(1)}, bf16[128,3584]{1,0:T(8,128)(2,1)S(1)}, u32[]{:S(2)}, u32[]{:S(2)}) collective-permute-start(bf16[128,3584]{1,0:T(8,128)(2,1)S(1)} %add.16), channel_id=1, source_target_pairs={{1,2},{2,1},{5,6},{6,5},{9,10},{10,9},{13,14},{14,13},{17,18},{18,... | collective-permute-start | bytes 2752520 | tf_op jit(solution)/shard_map/ppermute | solution.py:219
  288.2 25.7 %collective-permute-start.23 = (bf16[128,3584]{1,0:T(8,128)(2,1)S(1)}, bf16[128,3584]{1,0:T(8,128)(2,1)S(1)}, u32[]{:S(2)}, u32[]{:S(2)}) collective-permute-start(bf16[128,3584]{1,0:T(8,128)(2,1)S(1)} %add.18), channel_id=1, source_target_pairs={{1,3},{2,0},{5,7},{6,4},{9,11},{10,8},{13,15},{14,12},{17,19},{18,... | collective-permute-start | bytes 2752520 | tf_op jit(solution)/shard_map/ppermute | solution.py:219
  (19 other events, 106.4 us)
where the time goes:
time: 317 us
  waiting for transfers between devices  142 us (45%)
  Pallas kernels  103 us (32%)
  starting transfers between devices  61.3 us (19%)
  local copies, waits for them, and re-layouts  5.59 us (2%)
  other arithmetic  3.66 us (1%)
    pallas_call x13, Pallas kernels, call(): pl.pallas_call(kernel, in_specs=specs + [pl.BlockSpec(memory_space=pl.ANY...  103 us
    ppermute x10, waiting for transfers between devices, along(): return lax.ppermute(rows, 'local', pairs)  72.5 us
    ppermute x14, waiting for transfers between devices, give_back(): lax.ppermute(blocks[j], 'node', [(i, i ^ j) for i in range(count)])  39.1 us
    all_to_all x6, waiting for transfers between devices, over_nodes(): return lax.all_to_all(cut, 'node', 0, 0, tiled=True).reshape(rows.shape)  30.7 us
    ppermute x10, starting transfers between devices, along(): return lax.ppermute(rows, 'local', pairs)  24.5 us
    all_to_all x6, starting transfers between devices, over_nodes(): return lax.all_to_all(cut, 'node', 0, 0, tiled=True).reshape(rows.shape)  23.9 us
    ppermute x14, starting transfers between devices, give_back(): lax.ppermute(blocks[j], 'node', [(i, i ^ j) for i in range(count)])  12.8 us
  transfers between devices with their start and end apart: 30, of which 13 were waited for; matrix products, arithmetic and copies ran while one was open for 0% of the time, Pallas kernels for 32%

commit v1 on v0

--- a/solution.py
+++ b/solution.py
@@ -15,9 +15,9 @@
 
 LANES = 128
 WIDE = 512
-VMEM = 60 * 1024 * 1024
+VMEM = 62 * 1024 * 1024
+PARTS = 1
 PACE = 2000000000
-WHOLE = (2, 3)
 COSTS = {
     "route": 3, "dispatch0": 4, "dispatch1": 4, "dispatch2": 4, "dispatch3": 4,
     "experts0": 18, "experts1": 18, "experts2": 18, "experts3": 18,
@@ -93,10 +93,11 @@
     nodes, local_count, slots = sizes
     count = chunk[0].shape[0]
     width = (chunk[0].shape[1] - LANES) // 2
+    sources = len(chunk)
 
     def body(place_ref, *refs):
-        chunk_refs, (out_ref, picks_ref, xor_ref) = refs[:-3], refs[-3:]
-        node, local = place_ref[0], place_ref[1]
+        chunk_refs, (out_ref, picks_ref) = refs[:sources], refs[sources:]
+        local = place_ref[1]
 
         def tile(start, size):
             return functools.reduce(jnp.add, [c[:, start : start + size] for c in chunk_refs])
@@ -105,24 +106,20 @@
         second = lax.broadcasted_iota(jnp.int32, (count, count), 1)
         table = dot(tile(2 * width, LANES), (first == second).astype(jnp.bfloat16), ROWS)
         slot = lax.broadcasted_iota(jnp.int32, (slots, count), 0).astype(jnp.float32)
-
-        def choose(other):
-            wanted = (other * local_count + local).astype(jnp.float32)
+        picks, weighed = [], []
+        for j in range(nodes):
+            wanted = (j * local_count + local).astype(jnp.float32)
             pick = jnp.zeros((slots, count), jnp.float32)
             weigh = jnp.zeros((slots, count), jnp.float32)
             for k in range(top):
                 hit = (table[k : k + 1] == wanted) & (table[top + k : top + k + 1] == slot)
                 pick = jnp.where(hit, 1.0, pick)
                 weigh = jnp.where(hit, table[2 * top + k : 2 * top + k + 1], weigh)
-            return pick, weigh
-
-        def stack(parts):
-            return jnp.concatenate(parts, axis=0).astype(jnp.bfloat16)
-
-        chosen = [choose(jnp.int32(j)) for j in range(nodes)]
-        picks, weighed = stack([c[0] for c in chosen]), stack([c[1] for c in chosen])
+            picks.append(pick)
+            weighed.append(weigh)
+        picks = jnp.concatenate(picks, axis=0).astype(jnp.bfloat16)
+        weighed = jnp.concatenate(weighed, axis=0).astype(jnp.bfloat16)
         picks_ref[...] = picks
-        xor_ref[...] = stack([choose(jnp.bitwise_xor(node, j))[0] for j in range(nodes)])
         for start, size in columns(width):
             taken = dot(picks, tile(start, size))
             out_ref[:, start : start + size] = taken.astype(jnp.bfloat16)
@@ -133,21 +130,20 @@
         body,
         (place, *chunk),
         after,
-        [shape(nodes * slots, 2 * width)] + [shape(nodes * slots, count)] * 2,
+        [shape(nodes * slots, 2 * width), shape(nodes * slots, count)],
         f"dispatch{step}",
         [pl.BlockSpec(memory_space=pltpu.SMEM)]
-        + [pl.BlockSpec(memory_space=pltpu.VMEM)] * len(chunk),
-    )
-
-
-def experts(step, blocks, nodes, place, rows, w_gate, w_up, w_down, after):
+        + [pl.BlockSpec(memory_space=pltpu.VMEM)] * sources,
+    )
+
+
+def experts(step, rows, w_gate, w_up, w_down, after):
     count, wide = rows.shape
-    slots, width = count // nodes, wide // 2
+    width = wide // 2
     hidden = w_gate.shape[2]
     step_width = 512
 
-    def body(place_ref, rows_ref, gate_ref, up_ref, down_ref, *refs):
-        outs, sum_ref = refs[:blocks], refs[blocks]
+    def body(rows_ref, gate_ref, up_ref, down_ref, out_ref, sum_ref):
         step = pl.program_id(0)
 
         @pl.when(step == 0)
@@ -169,62 +165,69 @@
 
         @pl.when(step == pl.num_programs(0) - 1)
         def _():
-            if blocks == 1:
-                outs[0][...] = sum_ref[...].astype(jnp.bfloat16)
-            else:
-                for j in range(blocks):
-                    start = pl.multiple_of(jnp.bitwise_xor(place_ref[0], j) * slots, 8)
-                    outs[j][...] = sum_ref[pl.ds(start, slots), :].astype(jnp.bfloat16)
+            out_ref[...] = sum_ref[...].astype(jnp.bfloat16)
 
     across = pl.BlockSpec((1, width, step_width), lambda f: (0, 0, f))
     return call(
         body,
-        (place, rows, w_gate, w_up, w_down),
+        (rows, w_gate, w_up, w_down),
         after,
-        [shape(count // blocks, width)] * blocks,
+        shape(count, width),
         f"experts{step}",
         [
-            pl.BlockSpec(memory_space=pltpu.SMEM),
             pl.BlockSpec((count, wide), lambda f: (0, 0)),
             across,
             across,
             pl.BlockSpec((1, step_width, width), lambda f: (0, f, 0)),
         ],
         grid=(hidden // step_width,),
-        out_specs=[pl.BlockSpec((count // blocks, width), lambda f: (0, 0))] * blocks,
+        out_specs=pl.BlockSpec((count, width), lambda f: (0, 0)),
         scratch_shapes=[pltpu.VMEM((count, width), jnp.float32)],
     )
 
 
-def combine(step, blocks, picks, added, after):
-    nodes = len(blocks)
-    width = blocks[0].shape[1]
-
-    def body(*refs):
-        block_refs, picks_ref = refs[:nodes], refs[nodes]
-        added_refs, out_ref = refs[nodes + 1 : -1], refs[-1]
-        picks = picks_ref[...]
+def combine(step, rows, picks, after, part=0, parts=1):
+    count = rows.shape[0]
+    tokens, width = picks.shape[1], rows.shape[1] // parts
+
+    def body(rows_ref, picks_ref, out_ref):
         for start, size in columns(width):
-            rows = [b[:, start : start + size].astype(jnp.float32) for b in block_refs]
-            total = dot(picks, jnp.concatenate(rows, axis=0).astype(jnp.bfloat16), ROWS)
-            for other in added_refs:
-                total = total + other[:, start : start + size].astype(jnp.float32)
+            total = dot(picks_ref[...], rows_ref[:, start : start + size], ROWS)
             out_ref[:, start : start + size] = total.astype(jnp.bfloat16)
 
-    out = shape(picks.shape[1], width)
-    return call(body, (*blocks, picks, *added), after, out, f"combine{step}")
+    return call(
+        body,
+        (rows, picks),
+        after,
+        shape(tokens, width),
+        f"combine{step}",
+        [
+            pl.BlockSpec((count, width), lambda f: (0, part)),
+            pl.BlockSpec((count, tokens), lambda f: (0, 0)),
+        ],
+        grid=(1,),
+        out_specs=pl.BlockSpec((tokens, width), lambda f: (0, 0)),
+    )
+
+
+def tie(array, after):
+    def kernel(*refs):
+        del refs
+
+    anywhere = pl.BlockSpec(memory_space=pl.ANY)
+    return pl.pallas_call(
+        kernel,
+        in_specs=[anywhere] * (1 + len(after)),
+        out_specs=anywhere,
+        out_shape=jax.ShapeDtypeStruct(array.shape, array.dtype),
+        input_output_aliases={0: 0},
+        cost_estimate=pl.CostEstimate(flops=1, bytes_accessed=1, transcendentals=0),
+        name="tie",
+    )(array, *after)
 
 
 def along(rows, pairs):
     return lax.ppermute(rows, "local", pairs)
-
-
-def give_back(blocks):
-    count = len(blocks)
-    return [blocks[0]] + [
-        lax.ppermute(blocks[j], "node", [(i, i ^ j) for i in range(count)])
-        for j in range(1, count)
-    ]
 
 
 def per_device(expert_ids, gate_weights, tokens_in, grad_out, w_gate, w_up, w_down):
@@ -253,51 +256,54 @@
         (far, along(far, OUTWARD)),
     )
     last = ()
-    sent, picks, xors, back, sums = [[None] * 4 for _ in range(5)]
+    sent, picks, rows, back = [[None] * 4 for _ in range(4)]
 
     def send(k):
         nonlocal last
-        rows, picks[k], xors[k] = dispatch(k, sizes, top, place, chunks[k], last)
+        taken, picks[k] = dispatch(k, sizes, top, place, chunks[k], last)
         last = (picks[k],)
-        sent[k] = over_nodes(rows)
+        sent[k] = over_nodes(taken)
 
     def work(k):
         nonlocal last
-        count = 1 if k in WHOLE else node_count
-        out = experts(k, count, node_count, place, sent[k], w_gate, w_up, w_down, last)
-        last = (out[0],)
-        back[k] = [over_nodes(out[0])] if count == 1 else give_back(out)
-
-    def gather(k, *added):
+        rows[k] = experts(k, sent[k], w_gate, w_up, w_down, last)
+        last = (rows[k],)
+        return rows[k]
+
+    def give(k, *after):
+        back[k] = over_nodes(tie(rows[k], after) if after else rows[k])
+
+    def gather(k, part=0, parts=1):
         nonlocal last
-        chosen = picks[k] if k in WHOLE else xors[k]
-        sums[k] = combine(k, back[k], chosen, added, last)
-        last = (sums[k],)
-        return sums[k]
-
-    def late(array):
-        nonlocal last
-        last = last + (array,)
+        out = combine(k, back[k], picks[k], last, part, parts)
+        last = (out,)
+        return out
 
     send(0)
     send(1)
     work(0)
     send(2)
-    gather(0)
     work(1)
     send(3)
-    near = along(gather(1), NEAR)
     work(2)
-    late(near)
+    give(2)
     work(3)
-    across = along(gather(2), INWARD)
-    far = gather(3)
-    across = along(sums[2] + across, ACROSS)
-    outside = along(far + along(far, INWARD), OUTSIDE)
-    total = sums[0].astype(jnp.float32)
-    for part in (near, across, outside):
-        total = total + part.astype(jnp.float32)
-    return total.astype(jnp.bfloat16)
+    give(3)
+    middle = gather(2)
+    passed = along(middle, INWARD)
+    give(1, middle)
+    middle = middle + passed
+    last = last + (middle,)
+    far = [gather(3, part, PARTS) for part in range(PARTS)]
+    inward = [along(half, INWARD) for half in far]
+    first = gather(1)
+    near = along(first, NEAR)
+    give(0, first)
+    across = along(middle, ACROSS)
+    far = [along(half + other, OUTSIDE) for half, other in zip(far, inward)]
+    total = gather(0).astype(jnp.float32) + near.astype(jnp.float32) + across.astype(jnp.float32)
+    far = jnp.concatenate(far, axis=1)
+    return (total + far.astype(jnp.float32)).astype(jnp.bfloat16)
 
 
 def solution(mesh):

time: 317 us -> 306 us (0.965)
  starting transfers between devices: 61.3 us -> 54.2 us
  waiting for transfers between devices: 142 us -> 136 us
  other arithmetic: 3.66 us -> 8.68 us
  local copies, waits for them, and re-layouts: 5.59 us -> 2.22 us
    ppermute x14 -> x0, waiting for transfers between devices: 39.1 us -> none  [give_back(): lax.ppermute(blocks[j], 'node', [(i, i ^ j) for i in range(count)])]
    ppermute x10, waiting for transfers between devices: 72.5 us -> 91.6 us  [along(): return lax.ppermute(rows, 'local', pairs)]
    all_to_all x6 -> x8, waiting for transfers between devices: 30.7 us -> 44.7 us  [over_nodes(): return lax.all_to_all(cut, 'node', 0, 0, tiled=True).reshape(rows.shape)]
    ppermute x14 -> x0, starting transfers between devices: 12.8 us -> none  [give_back(): lax.ppermute(blocks[j], 'node', [(i, i ^ j) for i in range(count)])]
    all_to_all x6 -> x8, starting transfers between devices: 23.9 us -> 33.2 us  [over_nodes(): return lax.all_to_all(cut, 'node', 0, 0, tiled=True).reshape(rows.shape)]
    add x2, other arithmetic: 0.42 us -> 4.64 us  [the longest x1 2.33 us: per_device(): middle = middle + passed]
    ppermute x10, starting transfers between devices: 24.5 us -> 21.1 us  [along(): return lax.ppermute(rows, 'local', pairs)]
    unnamed x42 -> x12, local copies, waits for them, and re-layouts: 5.59 us -> 2.22 us
  transfers between devices with their start and end apart: 30 -> 18, of which waited for: 13 -> 11; matrix products, arithmetic and copies ran while one was open for 0% -> 2% of each run, Pallas kernels for 32% -> 33%
where the time goes in v1:
time: 306 us; the launch traced here: 305 us
  waiting for transfers between devices  136 us (44%)
  Pallas kernels  103 us (34%)
  starting transfers between devices  54.2 us (18%)
  other arithmetic  8.68 us (3%)
    pallas_call x13, Pallas kernels, call(): pl.pallas_call(kernel, in_specs=specs + [pl.BlockSpec(memory_space=pl.ANY...  103 us
    ppermute x10, waiting for transfers between devices, along(): return lax.ppermute(rows, 'local', pairs)  91.6 us
    all_to_all x8, waiting for transfers between devices, over_nodes(): return lax.all_to_all(cut, 'node', 0, 0, tiled=True).reshape(rows.shape)  44.7 us
    all_to_all x8, starting transfers between devices, over_nodes(): return lax.all_to_all(cut, 'node', 0, 0, tiled=True).reshape(rows.shape)  33.2 us
    ppermute x10, starting transfers between devices, along(): return lax.ppermute(rows, 'local', pairs)  21.1 us
  transfers between devices with their start and end apart: 18, of which 11 were waited for; matrix products, arithmetic and copies ran while one was open for 2% of the time, Pallas kernels for 33%

profile of v1, /device:TPU:0, one launch (start us, length us, event | category | flops | bytes accessed | tf_op | source)
XLA Modules:
  0.0 304.9 jit_solution(12718385024071226251)
XLA Ops:
  0.0 3.1 %route.1.refs_1_ = bf16[128,7296]{1,0:T(8,128)(2,1)} custom-call(s32[4,128]{1,0:T(4,128)} %bitcast.31, bf16[4,128]{1,0:T(4,128)(2,1)} %bitcast.32, bf16[128,3584]{1,0:T(8,128)(2,1)} %refs_2_.5, bf16[128,3584]{1,0:T(8,128)(2,1)} %refs_3_.5), custom_call_target="tpu_custom_call" | custom-call | flops 6000000000 | bytes 1000 | tf_op jit(solution)/shard_map/route/pallas_call | solution.py:43
  3.1 3.0 collective-permute-start
  7.5 4.2 %dispatch0.1 = (bf16[192,7168]{1,0:T(8,128)(2,1)}, bf16[192,128]{1,0:T(8,128)(2,1)}) custom-call(s32[2]{0:T(128)} %pad_add_fusion.refs_0_, bf16[128,7296]{1,0:T(8,128)(2,1)} %route.1.refs_1_), custom_call_target="tpu_custom_call" | custom-call | flops 8000000000 | bytes 1000 | tf_op jit(solution)/shard_map/dispatch0/pallas_call | solution.py:43
  11.7 4.4 %all-to-all-start = ((bf16[8,24,7168]{2,1,0:T(8,128)(2,1)}), bf16[8,24,7168]{2,1,0:T(8,128)(2,1)}, u32[]{:S(2)}, u32[]{:S(2)}) async-start(bf16[8,24,7168]{2,1,0:T(8,128)(2,1)} %bitcast.23), calls=%async_computation | async-start | bytes 5505024 | tf_op jit(solution)/shard_map/all_to_all | solution.py:245
  17.4 29.7 %collective-permute-done.refs_1_ = bf16[128,7296]{1,0:T(8,128)(2,1)} collective-permute-done((bf16[128,7296]{1,0:T(8,128)(2,1)}, bf16[128,7296]{1,0:T(8,128)(2,1)}, u32[]{:S(2)}, u32[]{:S(2)}) %collective-permute-start) | collective-permute-done | bytes 1867808 | tf_op jit(solution)/shard_map/ppermute | solution.py:230
  49.1 4.2 %dispatch1.1 = (bf16[192,7168]{1,0:T(8,128)(2,1)}, bf16[192,128]{1,0:T(8,128)(2,1)}) custom-call(s32[2]{0:T(128)} %pad_add_fusion.refs_0_, bf16[128,7296]{1,0:T(8,128)(2,1)} %collective-permute-done.refs_1_, bf16[192,128]{1,0:T(8,128)(2,1)} %get-tuple-element.14.refs_2_.refs_1_), custom_call_target="tpu_custom_call" | custom-call | flops 8000000000 | bytes 1000 | tf_op jit(solution)/shard_map/dispatch1/pallas_call | solution.py:43
  53.3 4.4 %all-to-all-start.1 = ((bf16[8,24,7168]{2,1,0:T(8,128)(2,1)}), bf16[8,24,7168]{2,1,0:T(8,128)(2,1)}, u32[]{:S(2)}, u32[]{:S(2)}) async-start(bf16[8,24,7168]{2,1,0:T(8,128)(2,1)} %bitcast.22), calls=%async_computation.1 | async-start | bytes 5505024 | tf_op jit(solution)/shard_map/all_to_all | solution.py:245
  57.7 17.9 %experts0.1.refs_3_.refs_0_ = bf16[192,3584]{1,0:T(8,128)(2,1)} custom-call(bf16[192,7168]{1,0:T(8,128)(2,1)} %bitcast.5.refs_0_, bf16[1,3584,1024]{2,1,0:T(8,128)(2,1)} %refs_1_.7, bf16[1,3584,1024]{2,1,0:T(8,128)(2,1)} %refs_2_.9, bf16[1,1024,3584]{2,1,0:T(8,128)(2,1)} %refs_3_.9, bf16[192,128]{1,0:T(8,128)(2,1)} %get-tuple-element.15.refs_4_.refs_1_), custom_call_target="tpu_custom_call" | custom-call | flops 35999997952 | bytes 1000 | tf_op jit(solution)/shard_map/experts0/pallas_call | solution.py:43
  76.9 16.2 %collective-permute-done.2.refs_2_ = bf16[128,7296]{1,0:T(8,128)(2,1)} collective-permute-done((bf16[128,7296]{1,0:T(8,128)(2,1)S(1)}, bf16[128,7296]{1,0:T(8,128)(2,1)}, u32[]{:S(2)}, u32[]{:S(2)}) %collective-permute-start.2) | collective-permute-done | bytes 1867808 | tf_op jit(solution)/shard_map/ppermute | solution.py:230
  93.1 4.7 %dispatch2.1 = (bf16[192,7168]{1,0:T(8,128)(2,1)}, bf16[192,128]{1,0:T(8,128)(2,1)}) custom-call(s32[2]{0:T(128)} %pad_add_fusion.refs_0_, bf16[128,7296]{1,0:T(8,128)(2,1)} %copy-done.5, bf16[128,7296]{1,0:T(8,128)(2,1)} %collective-permute-done.2.refs_2_, bf16[192,3584]{1,0:T(8,128)(2,1)} %experts0.1.refs_3_.refs_0_), custom_call_target="tpu_custom_call" | custom-call | flops 8000000000 | bytes 1000 | tf_op jit(solution)/shard_map/dispatch2/pallas_call | solution.py:43
  97.8 4.6 %all-to-all-start.2 = ((bf16[8,24,7168]{2,1,0:T(8,128)(2,1)}), bf16[8,24,7168]{2,1,0:T(8,128)(2,1)}, u32[]{:S(2)}, u32[]{:S(2)}) async-start(bf16[8,24,7168]{2,1,0:T(8,128)(2,1)} %bitcast.24), calls=%async_computation.2 | async-start | bytes 5505024 | tf_op jit(solution)/shard_map/all_to_all | solution.py:245
  102.4 17.9 %experts1.1.refs_3_.refs_0_ = bf16[192,3584]{1,0:T(8,128)(2,1)} custom-call(bf16[192,7168]{1,0:T(8,128)(2,1)} %bitcast.7.refs_0_, bf16[1,3584,1024]{2,1,0:T(8,128)(2,1)} %refs_1_.7, bf16[1,3584,1024]{2,1,0:T(8,128)(2,1)} %refs_2_.9, bf16[1,1024,3584]{2,1,0:T(8,128)(2,1)} %refs_3_.9, bf16[192,128]{1,0:T(8,128)(2,1)} %get-tuple-element.17.refs_4_.refs_1_), custom_call_target="tpu_custom_call" | custom-call | flops 35999997952 | bytes 1000 | tf_op jit(solution)/shard_map/experts1/pallas_call | solution.py:43
  120.3 18.5 %collective-permute-done.4.refs_2_ = bf16[128,7296]{1,0:T(8,128)(2,1)} collective-permute-done((bf16[128,7296]{1,0:T(8,128)(2,1)}, bf16[128,7296]{1,0:T(8,128)(2,1)}, u32[]{:S(2)}, u32[]{:S(2)}) %collective-permute-start.4) | collective-permute-done | bytes 1867808 | tf_op jit(solution)/shard_map/ppermute | solution.py:230
  138.8 4.7 %dispatch3.1 = (bf16[192,7168]{1,0:T(8,128)(2,1)}, bf16[192,128]{1,0:T(8,128)(2,1)}) custom-call(s32[2]{0:T(128)} %pad_add_fusion.refs_0_, bf16[128,7296]{1,0:T(8,128)(2,1)} %collective-permute-done.3.refs_1_, bf16[128,7296]{1,0:T(8,128)(2,1)} %collective-permute-done.4.refs_2_, bf16[192,3584]{1,0:T(8,128)(2,1)} %experts1.1.refs_3_.refs_0_), custom_call_target="tpu_custom_call" | custom-call | flops 8000000000 | bytes 1000 | tf_op jit(solution)/shard_map/dispatch3/pallas_call | solution.py:43
  143.5 4.4 %all-to-all-start.4 = ((bf16[8,24,7168]{2,1,0:T(8,128)(2,1)}), bf16[8,24,7168]{2,1,0:T(8,128)(2,1)}, u32[]{:S(2)}, u32[]{:S(2)}) async-start(bf16[8,24,7168]{2,1,0:T(8,128)(2,1)} %bitcast.25), calls=%async_computation.4 | async-start | bytes 5505024 | tf_op jit(solution)/shard_map/all_to_all | solution.py:245
  148.0 17.9 %experts2.1.refs_4_ = bf16[192,3584]{1,0:T(8,128)(2,1)} custom-call(bf16[192,7168]{1,0:T(8,128)(2,1)} %bitcast.9.refs_0_, bf16[1,3584,1024]{2,1,0:T(8,128)(2,1)} %refs_1_.7, bf16[1,3584,1024]{2,1,0:T(8,128)(2,1)} %refs_2_.9, bf16[1,1024,3584]{2,1,0:T(8,128)(2,1)} %refs_3_.9, bf16[192,128]{1,0:T(8,128)(2,1)} %get-tuple-element.19.refs_4_.refs_1_), custom_call_target="tpu_custom_call" | custom-call | flops 35999997952 | bytes 1000 | tf_op jit(solution)/shard_map/experts2/pallas_call | solution.py:43
  165.9 15.8 %all-to-all-done.4 = bf16[8,24,7168]{2,1,0:T(8,128)(2,1)} async-done(((bf16[8,24,7168]{2,1,0:T(8,128)(2,1)}), bf16[8,24,7168]{2,1,0:T(8,128)(2,1)}, u32[]{:S(2)}, u32[]{:S(2)}) %all-to-all-start.4) | async-done | bytes 2752544 | tf_op jit(solution)/shard_map/all_to_all | solution.py:245
  181.6 3.8 %all-to-all-start.3 = ((bf16[8,24,3584]{2,1,0:T(8,128)(2,1)}), bf16[8,24,3584]{2,1,0:T(8,128)(2,1)S(1)}, u32[]{:S(2)}, u32[]{:S(2)}) async-start(bf16[8,24,3584]{2,1,0:T(8,128)(2,1)} %bitcast.30), calls=%async_computation.3 | async-start | bytes 2752512 | tf_op jit(solution)/shard_map/all_to_all | solution.py:245
  185.4 17.9 %experts3.1.refs_2_ = bf16[192,3584]{1,0:T(8,128)(2,1)} custom-call(bf16[192,7168]{1,0:T(8,128)(2,1)} %bitcast.13.refs_0_, bf16[1,3584,1024]{2,1,0:T(8,128)(2,1)} %refs_1_.7, bf16[1,3584,1024]{2,1,0:T(8,128)(2,1)} %refs_2_.9, bf16[1,1024,3584]{2,1,0:T(8,128)(2,1)} %refs_3_.9, bf16[192,3584]{1,0:T(8,128)(2,1)} %experts2.1.refs_4_), custom_call_target="tpu_custom_call" | custom-call | flops 35999997952 | bytes 1000 | tf_op jit(solution)/shard_map/experts3/pallas_call | solution.py:43
  205.2 3.6 %all-to-all-start.6 = ((bf16[8,24,3584]{2,1,0:T(8,128)(2,1)}), bf16[8,24,3584]{2,1,0:T(8,128)(2,1)S(1)}, u32[]{:S(2)}, u32[]{:S(2)}) async-start(bf16[8,24,3584]{2,1,0:T(8,128)(2,1)} %bitcast.28), calls=%async_computation.6 | async-start | bytes 2752512 | tf_op jit(solution)/shard_map/all_to_all | solution.py:245
  211.5 2.8 collective-permute-start.5
  214.3 13.3 %all-to-all-done.6 = bf16[8,24,3584]{2,1,0:T(8,128)(2,1)S(1)} async-done(((bf16[8,24,3584]{2,1,0:T(8,128)(2,1)}), bf16[8,24,3584]{2,1,0:T(8,128)(2,1)S(1)}, u32[]{:S(2)}, u32[]{:S(2)}) %all-to-all-start.6) | async-done | bytes 1376288 | tf_op jit(solution)/shard_map/all_to_all | solution.py:245
  227.6 4.3 %all-to-all-start.5 = ((bf16[8,24,3584]{2,1,0:T(8,128)(2,1)}), bf16[8,24,3584]{2,1,0:T(8,128)(2,1)}, u32[]{:S(2)}, u32[]{:S(2)}) async-start(bf16[8,24,3584]{2,1,0:T(8,128)(2,1)} %bitcast.21), calls=%async_computation.5 | async-start | bytes 2752512 | tf_op jit(solution)/shard_map/all_to_all | solution.py:245
  238.8 5.3 %collective-permute-start.8 = (bf16[128,3584]{1,0:T(8,128)(2,1)}, bf16[128,3584]{1,0:T(8,128)(2,1)}, u32[]{:S(2)}, u32[]{:S(2)}) collective-permute-start(bf16[128,3584]{1,0:T(8,128)(2,1)} %combine3.1.refs_2_), channel_id=1, source_target_pairs={{0,1},{3,2},{4,5},{7,6},{8,9},{11,10},{12,13},{15,14},{16,17},{19,... | collective-permute-start | bytes 2752520 | tf_op jit(solution)/shard_map/ppermute | solution.py:230
  244.2 6.6 %all-to-all-done.5 = bf16[8,24,3584]{2,1,0:T(8,128)(2,1)} async-done(((bf16[8,24,3584]{2,1,0:T(8,128)(2,1)}), bf16[8,24,3584]{2,1,0:T(8,128)(2,1)}, u32[]{:S(2)}, u32[]{:S(2)}) %all-to-all-start.5) | async-done | bytes 1376288 | tf_op jit(solution)/shard_map/all_to_all | solution.py:245
  250.8 2.7 combine1.1.refs_1_.refs_2_
  253.5 3.7 %all-to-all-start.7 = ((bf16[8,24,3584]{2,1,0:T(8,128)(2,1)}), bf16[8,24,3584]{2,1,0:T(8,128)(2,1)S(1)}, u32[]{:S(2)}, u32[]{:S(2)}) async-start(bf16[8,24,3584]{2,1,0:T(8,128)(2,1)} %bitcast.20), calls=%async_computation.7 | async-start | bytes 2752512 | tf_op jit(solution)/shard_map/all_to_all | solution.py:245
  260.6 3.7 %collective-permute-done.8 = bf16[128,3584]{1,0:T(8,128)(2,1)} collective-permute-done((bf16[128,3584]{1,0:T(8,128)(2,1)}, bf16[128,3584]{1,0:T(8,128)(2,1)}, u32[]{:S(2)}, u32[]{:S(2)}) %collective-permute-start.8) | collective-permute-done | bytes 917536 | tf_op jit(solution)/shard_map/ppermute | solution.py:230
  267.9 8.2 %all-to-all-done.7 = bf16[8,24,3584]{2,1,0:T(8,128)(2,1)S(1)} async-done(((bf16[8,24,3584]{2,1,0:T(8,128)(2,1)}), bf16[8,24,3584]{2,1,0:T(8,128)(2,1)S(1)}, u32[]{:S(2)}, u32[]{:S(2)}) %all-to-all-start.7) | async-done | bytes 1376288 | tf_op jit(solution)/shard_map/all_to_all | solution.py:245
  277.2 2.7 combine0.1
  279.9 21.5 %collective-permute-done.6 = bf16[128,3584]{1,0:T(8,128)(2,1)} collective-permute-done((bf16[128,3584]{1,0:T(8,128)(2,1)}, bf16[128,3584]{1,0:T(8,128)(2,1)}, u32[]{:S(2)}, u32[]{:S(2)}) %collective-permute-start.6) | collective-permute-done | bytes 917536 | tf_op jit(solution)/shard_map/ppermute | solution.py:230
  301.5 3.4 %add_convert_fusion = bf16[128,3584]{1,0:T(8,128)(2,1)} fusion(bf16[128,3584]{1,0:T(8,128)(2,1)} %collective-permute-done.9, bf16[128,3584]{1,0:T(8,128)(2,1)} %collective-permute-done.7, bf16[128,3584]{1,0:T(8,128)(2,1)} %collective-permute-done.6, bf16[128,3584]{1,0:T(8,128)(2,1)} %combine0.1), kind=kLoop, calls=%fused_computation | loop fusion | flops 3670016 | bytes 4587520 | tf_op jit(solution)/shard_map/convert_element_type | solution.py:306
  (35 shorter events, 25.6 us)
Async XLA Ops:
  3.1 44.1 %collective-permute-start = (bf16[128,7296]{1,0:T(8,128)(2,1)}, bf16[128,7296]{1,0:T(8,128)(2,1)}, u32[]{:S(2)}, u32[]{:S(2)}) collective-permute-start(bf16[128,7296]{1,0:T(8,128)(2,1)} %route.1.refs_1_), channel_id=1, source_target_pairs={{0,1},{1,0},{2,3},{3,2},{4,5},{5,4},{6,7},{7,6},{8,9},{9,8},{10,11... | collective-permute-start | bytes 5603336 | tf_op jit(solution)/shard_map/ppermute | solution.py:230
  6.1 10.0 %collective-permute-start.1 = (bf16[128,7296]{1,0:T(8,128)(2,1)}, bf16[128,7296]{1,0:T(8,128)(2,1)S(1)}, u32[]{:S(2)}, u32[]{:S(2)}) collective-permute-start(bf16[128,7296]{1,0:T(8,128)(2,1)} %route.1.refs_1_), channel_id=1, source_target_pairs={{1,2},{2,1},{5,6},{6,5},{9,10},{10,9},{13,14},{14,13},{17,18},{18,... | collective-permute-start | bytes 5603336 | tf_op jit(solution)/shard_map/ppermute | solution.py:230
  11.7 41.6 %all-to-all-start = ((bf16[8,24,7168]{2,1,0:T(8,128)(2,1)}), bf16[8,24,7168]{2,1,0:T(8,128)(2,1)}, u32[]{:S(2)}, u32[]{:S(2)}) async-start(bf16[8,24,7168]{2,1,0:T(8,128)(2,1)} %bitcast.23), calls=%async_computation | async-start | bytes 5505024 | tf_op jit(solution)/shard_map/all_to_all | solution.py:245
  16.1 37.1 %copy-start.5 = (bf16[128,7296]{1,0:T(8,128)(2,1)}, bf16[128,7296]{1,0:T(8,128)(2,1)S(1)}, u32[]{:S(2)}) copy-start(bf16[128,7296]{1,0:T(8,128)(2,1)S(1)} %collective-permute-done.1.refs_1_) | copy-start | bytes 5603332
  16.1 76.9 %collective-permute-start.2 = (bf16[128,7296]{1,0:T(8,128)(2,1)S(1)}, bf16[128,7296]{1,0:T(8,128)(2,1)}, u32[]{:S(2)}, u32[]{:S(2)}) collective-permute-start(bf16[128,7296]{1,0:T(8,128)(2,1)S(1)} %collective-permute-done.1.refs_1_), channel_id=1, source_target_pairs={{1,0},{2,3},{5,4},{6,7},{9,8},{10,11},{13,12},{14,15},{17,16},{18,... | collective-permute-start | bytes 5603336 | tf_op jit(solution)/shard_map/ppermute | solution.py:230
  47.1 28.4 %collective-permute-start.3 = (bf16[128,7296]{1,0:T(8,128)(2,1)}, bf16[128,7296]{1,0:T(8,128)(2,1)}, u32[]{:S(2)}, u32[]{:S(2)}) collective-permute-start(bf16[128,7296]{1,0:T(8,128)(2,1)} %collective-permute-done.refs_1_), channel_id=1, source_target_pairs={{1,2},{2,1},{5,6},{6,5},{9,10},{10,9},{13,14},{14,13},{17,18},{18,... | collective-permute-start | bytes 5603336 | tf_op jit(solution)/shard_map/ppermute | solution.py:230
  53.3 44.5 %all-to-all-start.1 = ((bf16[8,24,7168]{2,1,0:T(8,128)(2,1)}), bf16[8,24,7168]{2,1,0:T(8,128)(2,1)}, u32[]{:S(2)}, u32[]{:S(2)}) async-start(bf16[8,24,7168]{2,1,0:T(8,128)(2,1)} %bitcast.22), calls=%async_computation.1 | async-start | bytes 5505024 | tf_op jit(solution)/shard_map/all_to_all | solution.py:245
  75.6 63.2 %collective-permute-start.4 = (bf16[128,7296]{1,0:T(8,128)(2,1)}, bf16[128,7296]{1,0:T(8,128)(2,1)}, u32[]{:S(2)}, u32[]{:S(2)}) collective-permute-start(bf16[128,7296]{1,0:T(8,128)(2,1)} %collective-permute-done.3.refs_1_), channel_id=1, source_target_pairs={{1,0},{2,3},{5,4},{6,7},{9,8},{10,11},{13,12},{14,15},{17,16},{18,... | collective-permute-start | bytes 5603336 | tf_op jit(solution)/shard_map/ppermute | solution.py:230
  97.8 45.8 %all-to-all-start.2 = ((bf16[8,24,7168]{2,1,0:T(8,128)(2,1)}), bf16[8,24,7168]{2,1,0:T(8,128)(2,1)}, u32[]{:S(2)}, u32[]{:S(2)}) async-start(bf16[8,24,7168]{2,1,0:T(8,128)(2,1)} %bitcast.24), calls=%async_computation.2 | async-start | bytes 5505024 | tf_op jit(solution)/shard_map/all_to_all | solution.py:245
  143.5 38.1 %all-to-all-start.4 = ((bf16[8,24,7168]{2,1,0:T(8,128)(2,1)}), bf16[8,24,7168]{2,1,0:T(8,128)(2,1)}, u32[]{:S(2)}, u32[]{:S(2)}) async-start(bf16[8,24,7168]{2,1,0:T(8,128)(2,1)} %bitcast.25), calls=%async_computation.4 | async-start | bytes 5505024 | tf_op jit(solution)/shard_map/all_to_all | solution.py:245
  181.6 22.4 %all-to-all-start.3 = ((bf16[8,24,3584]{2,1,0:T(8,128)(2,1)}), bf16[8,24,3584]{2,1,0:T(8,128)(2,1)S(1)}, u32[]{:S(2)}, u32[]{:S(2)}) async-start(bf16[8,24,3584]{2,1,0:T(8,128)(2,1)} %bitcast.30), calls=%async_computation.3 | async-start | bytes 2752512 | tf_op jit(solution)/shard_map/all_to_all | solution.py:245
  204.1 1.1 copy-start.3
  205.2 22.4 %all-to-all-start.6 = ((bf16[8,24,3584]{2,1,0:T(8,128)(2,1)}), bf16[8,24,3584]{2,1,0:T(8,128)(2,1)S(1)}, u32[]{:S(2)}, u32[]{:S(2)}) async-start(bf16[8,24,3584]{2,1,0:T(8,128)(2,1)} %bitcast.28), calls=%async_computation.6 | async-start | bytes 2752512 | tf_op jit(solution)/shard_map/all_to_all | solution.py:245
  211.5 22.3 %collective-permute-start.5 = (bf16[128,3584]{1,0:T(8,128)(2,1)}, bf16[128,3584]{1,0:T(8,128)(2,1)}, u32[]{:S(2)}, u32[]{:S(2)}) collective-permute-start(bf16[128,3584]{1,0:T(8,128)(2,1)} %combine2.1.refs_1_.refs_2_), channel_id=1, source_target_pairs={{0,1},{3,2},{4,5},{7,6},{8,9},{11,10},{12,13},{15,14},{16,17},{19,... | collective-permute-start | bytes 2752520 | tf_op jit(solution)/shard_map/ppermute | solution.py:230
  214.3 19.6 %copy-start = (bf16[128,3584]{1,0:T(8,128)(2,1)S(1)}, bf16[128,3584]{1,0:T(8,128)(2,1)}, u32[]{:S(2)}) copy-start(bf16[128,3584]{1,0:T(8,128)(2,1)} %combine2.1.refs_1_.refs_2_) | copy-start | bytes 2752516
  227.6 8.5 %copy-start.1 = (bf16[8,24,3584]{2,1,0:T(8,128)(2,1)}, bf16[8,24,3584]{2,1,0:T(8,128)(2,1)S(1)}, u32[]{:S(2)}) copy-start(bf16[8,24,3584]{2,1,0:T(8,128)(2,1)S(1)} %all-to-all-done.6) | copy-start | bytes 4128772
  227.6 23.2 %all-to-all-start.5 = ((bf16[8,24,3584]{2,1,0:T(8,128)(2,1)}), bf16[8,24,3584]{2,1,0:T(8,128)(2,1)}, u32[]{:S(2)}, u32[]{:S(2)}) async-start(bf16[8,24,3584]{2,1,0:T(8,128)(2,1)} %bitcast.21), calls=%async_computation.5 | async-start | bytes 2752512 | tf_op jit(solution)/shard_map/all_to_all | solution.py:245
  238.8 25.5 %collective-permute-start.8 = (bf16[128,3584]{1,0:T(8,128)(2,1)}, bf16[128,3584]{1,0:T(8,128)(2,1)}, u32[]{:S(2)}, u32[]{:S(2)}) collective-permute-start(bf16[128,3584]{1,0:T(8,128)(2,1)} %combine3.1.refs_2_), channel_id=1, source_target_pairs={{0,1},{3,2},{4,5},{7,6},{8,9},{11,10},{12,13},{15,14},{16,17},{19,... | collective-permute-start | bytes 2752520 | tf_op jit(solution)/shard_map/ppermute | solution.py:230
  253.5 10.8 %copy-start.4 = (bf16[128,3584]{1,0:T(8,128)(2,1)S(1)}, bf16[128,3584]{1,0:T(8,128)(2,1)}, u32[]{:S(2)}) copy-start(bf16[128,3584]{1,0:T(8,128)(2,1)} %combine3.1.refs_2_) | copy-start | bytes 2752516
  253.5 22.6 %all-to-all-start.7 = ((bf16[8,24,3584]{2,1,0:T(8,128)(2,1)}), bf16[8,24,3584]{2,1,0:T(8,128)(2,1)S(1)}, u32[]{:S(2)}, u32[]{:S(2)}) async-start(bf16[8,24,3584]{2,1,0:T(8,128)(2,1)} %bitcast.20), calls=%async_computation.7 | async-start | bytes 2752512 | tf_op jit(solution)/shard_map/all_to_all | solution.py:245
  257.3 22.7 %collective-permute-start.7 = (bf16[128,3584]{1,0:T(8,128)(2,1)}, bf16[128,3584]{1,0:T(8,128)(2,1)}, u32[]{:S(2)}, u32[]{:S(2)}) collective-permute-start(bf16[128,3584]{1,0:T(8,128)(2,1)} %add.15.refs_3_), channel_id=1, source_target_pairs={{1,2},{2,1},{5,6},{6,5},{9,10},{10,9},{13,14},{14,13},{17,18},{18,... | collective-permute-start | bytes 2752520 | tf_op jit(solution)/shard_map/ppermute | solution.py:230
  258.8 42.6 %collective-permute-start.6 = (bf16[128,3584]{1,0:T(8,128)(2,1)}, bf16[128,3584]{1,0:T(8,128)(2,1)}, u32[]{:S(2)}, u32[]{:S(2)}) collective-permute-start(bf16[128,3584]{1,0:T(8,128)(2,1)} %combine1.1.refs_1_.refs_2_), channel_id=1, source_target_pairs={{0,1},{1,0},{2,3},{3,2},{4,5},{5,4},{6,7},{7,6},{8,9},{9,8},{10,11... | collective-permute-start | bytes 2752520 | tf_op jit(solution)/shard_map/ppermute | solution.py:230
  266.6 34.8 %collective-permute-start.9 = (bf16[128,3584]{1,0:T(8,128)(2,1)}, bf16[128,3584]{1,0:T(8,128)(2,1)}, u32[]{:S(2)}, u32[]{:S(2)}) collective-permute-start(bf16[128,3584]{1,0:T(8,128)(2,1)} %add.18), channel_id=1, source_target_pairs={{1,3},{2,0},{5,7},{6,4},{9,11},{10,8},{13,15},{14,12},{17,19},{18,... | collective-permute-start | bytes 2752520 | tf_op jit(solution)/shard_map/ppermute | solution.py:230
  276.1 1.1 copy-start.2

commit v2 on v1

--- a/solution.py
+++ b/solution.py
@@ -19,7 +19,7 @@
 PARTS = 1
 PACE = 2000000000
 COSTS = {
-    "route": 3, "dispatch0": 4, "dispatch1": 4, "dispatch2": 4, "dispatch3": 4,
+    "add": 0.001, "route": 3, "dispatch0": 4, "dispatch1": 4, "dispatch2": 4, "dispatch3": 4,
     "experts0": 18, "experts1": 18, "experts2": 18, "experts3": 18,
     "combine0": 3, "combine1": 3, "combine2": 3, "combine3": 3,
 }
@@ -226,6 +226,17 @@
     )(array, *after)
 
 
+def add(*arrays):
+    def body(*refs):
+        for start, size in columns(arrays[0].shape[1]):
+            parts = [r[:, start : start + size].astype(jnp.float32) for r in refs[:-1]]
+            refs[-1][:, start : start + size] = functools.reduce(jnp.add, parts).astype(
+                jnp.bfloat16
+            )
+
+    return call(body, arrays, (), shape(*arrays[0].shape), "add")
+
+
 def along(rows, pairs):
     return lax.ppermute(rows, "local", pairs)
 
@@ -292,7 +303,7 @@
     middle = gather(2)
     passed = along(middle, INWARD)
     give(1, middle)
-    middle = middle + passed
+    middle = add(middle, passed)
     last = last + (middle,)
     far = [gather(3, part, PARTS) for part in range(PARTS)]
     inward = [along(half, INWARD) for half in far]
@@ -300,10 +311,8 @@
     near = along(first, NEAR)
     give(0, first)
     across = along(middle, ACROSS)
-    far = [along(half + other, OUTSIDE) for half, other in zip(far, inward)]
-    total = gather(0).astype(jnp.float32) + near.astype(jnp.float32) + across.astype(jnp.float32)
-    far = jnp.concatenate(far, axis=1)
-    return (total + far.astype(jnp.float32)).astype(jnp.bfloat16)
+    far = [along(add(half, other), OUTSIDE) for half, other in zip(far, inward)]
+    return add(gather(0), near, across, *far)
 
 
 def solution(mesh):

time: 306 us -> 306 us (level)
  Pallas kernels: 103 us -> 112 us
  other arithmetic: 8.68 us -> 0.59 us
    pallas_call x13 -> x16, Pallas kernels: 103 us -> 112 us  [call(): pl.pallas_call(kernel, in_specs=specs + [pl.BlockSpec(memory_space=pl.ANY...]
    add x2 -> x0, other arithmetic: 4.64 us -> none  [the longest x1 2.33 us: per_device(): middle = middle + passed]
    convert_element_type x1 -> x0, other arithmetic: 3.38 us -> none  [per_device(): return (total + far.astype(jnp.float32)).astype(jnp.bfloat16)]
  transfers between devices with their start and end apart: 18 -> 18, of which waited for: 11 -> 11; matrix products, arithmetic and copies ran while one was open for 2% -> 0% of each run, Pallas kernels for 33% -> 35%
where the time goes in v2:
time: 306 us; the launch traced here: 305 us
  waiting for transfers between devices  136 us (44%)
  Pallas kernels  112 us (37%)
  starting transfers between devices  54.2 us (18%)
    pallas_call x16, Pallas kernels, call(): pl.pallas_call(kernel, in_specs=specs + [pl.BlockSpec(memory_space=pl.ANY...  112 us
    ppermute x10, waiting for transfers between devices, along(): return lax.ppermute(rows, 'local', pairs)  92.2 us
    all_to_all x8, waiting for transfers between devices, over_nodes(): return lax.all_to_all(cut, 'node', 0, 0, tiled=True).reshape(rows.shape)  43.6 us
    all_to_all x8, starting transfers between devices, over_nodes(): return lax.all_to_all(cut, 'node', 0, 0, tiled=True).reshape(rows.shape)  33 us
    ppermute x10, starting transfers between devices, along(): return lax.ppermute(rows, 'local', pairs)  21.1 us
  transfers between devices with their start and end apart: 18, of which 11 were waited for; matrix products, arithmetic and copies ran while one was open for 0% of the time, Pallas kernels for 35%

profile of v2, /device:TPU:0, one launch (start us, length us, event | category | flops | bytes accessed | tf_op | source)
XLA Modules:
  0.0 304.7 jit_solution(6721831661087288050)
XLA Ops:
  0.0 3.1 %route.1.refs_1_ = bf16[128,7296]{1,0:T(8,128)(2,1)} custom-call(s32[4,128]{1,0:T(4,128)} %bitcast.31, bf16[4,128]{1,0:T(4,128)(2,1)} %bitcast.32, bf16[128,3584]{1,0:T(8,128)(2,1)} %refs_2_.5, bf16[128,3584]{1,0:T(8,128)(2,1)} %refs_3_.5), custom_call_target="tpu_custom_call" | custom-call | flops 6000000000 | bytes 1000 | tf_op jit(solution)/shard_map/route/pallas_call | solution.py:43
  3.1 3.0 collective-permute-start
  7.5 4.2 %dispatch0.1 = (bf16[192,7168]{1,0:T(8,128)(2,1)}, bf16[192,128]{1,0:T(8,128)(2,1)}) custom-call(s32[2]{0:T(128)} %pad_add_fusion.refs_0_, bf16[128,7296]{1,0:T(8,128)(2,1)} %route.1.refs_1_), custom_call_target="tpu_custom_call" | custom-call | flops 8000000000 | bytes 1000 | tf_op jit(solution)/shard_map/dispatch0/pallas_call | solution.py:43
  11.6 4.4 %all-to-all-start = ((bf16[8,24,7168]{2,1,0:T(8,128)(2,1)}), bf16[8,24,7168]{2,1,0:T(8,128)(2,1)}, u32[]{:S(2)}, u32[]{:S(2)}) async-start(bf16[8,24,7168]{2,1,0:T(8,128)(2,1)} %bitcast.23), calls=%async_computation | async-start | bytes 5505024 | tf_op jit(solution)/shard_map/all_to_all | solution.py:256
  17.4 29.8 %collective-permute-done.refs_1_ = bf16[128,7296]{1,0:T(8,128)(2,1)} collective-permute-done((bf16[128,7296]{1,0:T(8,128)(2,1)}, bf16[128,7296]{1,0:T(8,128)(2,1)}, u32[]{:S(2)}, u32[]{:S(2)}) %collective-permute-start) | collective-permute-done | bytes 1867808 | tf_op jit(solution)/shard_map/ppermute | solution.py:241
  49.1 4.2 %dispatch1.1 = (bf16[192,7168]{1,0:T(8,128)(2,1)}, bf16[192,128]{1,0:T(8,128)(2,1)}) custom-call(s32[2]{0:T(128)} %pad_add_fusion.refs_0_, bf16[128,7296]{1,0:T(8,128)(2,1)} %collective-permute-done.refs_1_, bf16[192,128]{1,0:T(8,128)(2,1)} %get-tuple-element.14.refs_2_.refs_1_), custom_call_target="tpu_custom_call" | custom-call | flops 8000000000 | bytes 1000 | tf_op jit(solution)/shard_map/dispatch1/pallas_call | solution.py:43
  53.3 4.4 %all-to-all-start.1 = ((bf16[8,24,7168]{2,1,0:T(8,128)(2,1)}), bf16[8,24,7168]{2,1,0:T(8,128)(2,1)}, u32[]{:S(2)}, u32[]{:S(2)}) async-start(bf16[8,24,7168]{2,1,0:T(8,128)(2,1)} %bitcast.22), calls=%async_computation.1 | async-start | bytes 5505024 | tf_op jit(solution)/shard_map/all_to_all | solution.py:256
  57.7 17.9 %experts0.1.refs_3_.refs_0_ = bf16[192,3584]{1,0:T(8,128)(2,1)} custom-call(bf16[192,7168]{1,0:T(8,128)(2,1)} %bitcast.5.refs_0_, bf16[1,3584,1024]{2,1,0:T(8,128)(2,1)} %refs_1_.7, bf16[1,3584,1024]{2,1,0:T(8,128)(2,1)} %refs_2_.9, bf16[1,1024,3584]{2,1,0:T(8,128)(2,1)} %refs_3_.9, bf16[192,128]{1,0:T(8,128)(2,1)} %get-tuple-element.15.refs_4_.refs_1_), custom_call_target="tpu_custom_call" | custom-call | flops 35999997952 | bytes 1000 | tf_op jit(solution)/shard_map/experts0/pallas_call | solution.py:43
  76.8 16.3 %collective-permute-done.2.refs_2_ = bf16[128,7296]{1,0:T(8,128)(2,1)} collective-permute-done((bf16[128,7296]{1,0:T(8,128)(2,1)S(1)}, bf16[128,7296]{1,0:T(8,128)(2,1)}, u32[]{:S(2)}, u32[]{:S(2)}) %collective-permute-start.2) | collective-permute-done | bytes 1867808 | tf_op jit(solution)/shard_map/ppermute | solution.py:241
  93.1 4.7 %dispatch2.1 = (bf16[192,7168]{1,0:T(8,128)(2,1)}, bf16[192,128]{1,0:T(8,128)(2,1)}) custom-call(s32[2]{0:T(128)} %pad_add_fusion.refs_0_, bf16[128,7296]{1,0:T(8,128)(2,1)} %copy-done.3, bf16[128,7296]{1,0:T(8,128)(2,1)} %collective-permute-done.2.refs_2_, bf16[192,3584]{1,0:T(8,128)(2,1)} %experts0.1.refs_3_.refs_0_), custom_call_target="tpu_custom_call" | custom-call | flops 8000000000 | bytes 1000 | tf_op jit(solution)/shard_map/dispatch2/pallas_call | solution.py:43
  97.8 4.6 %all-to-all-start.2 = ((bf16[8,24,7168]{2,1,0:T(8,128)(2,1)}), bf16[8,24,7168]{2,1,0:T(8,128)(2,1)}, u32[]{:S(2)}, u32[]{:S(2)}) async-start(bf16[8,24,7168]{2,1,0:T(8,128)(2,1)} %bitcast.24), calls=%async_computation.2 | async-start | bytes 5505024 | tf_op jit(solution)/shard_map/all_to_all | solution.py:256
  102.4 17.9 %experts1.1.refs_3_.refs_0_ = bf16[192,3584]{1,0:T(8,128)(2,1)} custom-call(bf16[192,7168]{1,0:T(8,128)(2,1)} %bitcast.7.refs_0_, bf16[1,3584,1024]{2,1,0:T(8,128)(2,1)} %refs_1_.7, bf16[1,3584,1024]{2,1,0:T(8,128)(2,1)} %refs_2_.9, bf16[1,1024,3584]{2,1,0:T(8,128)(2,1)} %refs_3_.9, bf16[192,128]{1,0:T(8,128)(2,1)} %get-tuple-element.17.refs_4_.refs_1_), custom_call_target="tpu_custom_call" | custom-call | flops 35999997952 | bytes 1000 | tf_op jit(solution)/shard_map/experts1/pallas_call | solution.py:43
  120.3 18.5 %collective-permute-done.4.refs_2_ = bf16[128,7296]{1,0:T(8,128)(2,1)} collective-permute-done((bf16[128,7296]{1,0:T(8,128)(2,1)}, bf16[128,7296]{1,0:T(8,128)(2,1)}, u32[]{:S(2)}, u32[]{:S(2)}) %collective-permute-start.4) | collective-permute-done | bytes 1867808 | tf_op jit(solution)/shard_map/ppermute | solution.py:241
  138.8 4.7 %dispatch3.1 = (bf16[192,7168]{1,0:T(8,128)(2,1)}, bf16[192,128]{1,0:T(8,128)(2,1)}) custom-call(s32[2]{0:T(128)} %pad_add_fusion.refs_0_, bf16[128,7296]{1,0:T(8,128)(2,1)} %collective-permute-done.3.refs_1_, bf16[128,7296]{1,0:T(8,128)(2,1)} %collective-permute-done.4.refs_2_, bf16[192,3584]{1,0:T(8,128)(2,1)} %experts1.1.refs_3_.refs_0_), custom_call_target="tpu_custom_call" | custom-call | flops 8000000000 | bytes 1000 | tf_op jit(solution)/shard_map/dispatch3/pallas_call | solution.py:43
  143.5 4.4 %all-to-all-start.4 = ((bf16[8,24,7168]{2,1,0:T(8,128)(2,1)}), bf16[8,24,7168]{2,1,0:T(8,128)(2,1)}, u32[]{:S(2)}, u32[]{:S(2)}) async-start(bf16[8,24,7168]{2,1,0:T(8,128)(2,1)} %bitcast.25), calls=%async_computation.4 | async-start | bytes 5505024 | tf_op jit(solution)/shard_map/all_to_all | solution.py:256
  148.0 17.9 %experts2.1.refs_4_ = bf16[192,3584]{1,0:T(8,128)(2,1)} custom-call(bf16[192,7168]{1,0:T(8,128)(2,1)} %bitcast.9.refs_0_, bf16[1,3584,1024]{2,1,0:T(8,128)(2,1)} %refs_1_.7, bf16[1,3584,1024]{2,1,0:T(8,128)(2,1)} %refs_2_.9, bf16[1,1024,3584]{2,1,0:T(8,128)(2,1)} %refs_3_.9, bf16[192,128]{1,0:T(8,128)(2,1)} %get-tuple-element.19.refs_4_.refs_1_), custom_call_target="tpu_custom_call" | custom-call | flops 35999997952 | bytes 1000 | tf_op jit(solution)/shard_map/experts2/pallas_call | solution.py:43
  165.9 15.8 %all-to-all-done.4 = bf16[8,24,7168]{2,1,0:T(8,128)(2,1)} async-done(((bf16[8,24,7168]{2,1,0:T(8,128)(2,1)}), bf16[8,24,7168]{2,1,0:T(8,128)(2,1)}, u32[]{:S(2)}, u32[]{:S(2)}) %all-to-all-start.4) | async-done | bytes 2752544 | tf_op jit(solution)/shard_map/all_to_all | solution.py:256
  181.7 3.8 %all-to-all-start.3 = ((bf16[8,24,3584]{2,1,0:T(8,128)(2,1)}), bf16[8,24,3584]{2,1,0:T(8,128)(2,1)S(1)}, u32[]{:S(2)}, u32[]{:S(2)}) async-start(bf16[8,24,3584]{2,1,0:T(8,128)(2,1)} %bitcast.30), calls=%async_computation.3 | async-start | bytes 2752512 | tf_op jit(solution)/shard_map/all_to_all | solution.py:256
  185.5 17.9 %experts3.1.refs_2_ = bf16[192,3584]{1,0:T(8,128)(2,1)} custom-call(bf16[192,7168]{1,0:T(8,128)(2,1)} %bitcast.13.refs_0_, bf16[1,3584,1024]{2,1,0:T(8,128)(2,1)} %refs_1_.7, bf16[1,3584,1024]{2,1,0:T(8,128)(2,1)} %refs_2_.9, bf16[1,1024,3584]{2,1,0:T(8,128)(2,1)} %refs_3_.9, bf16[192,3584]{1,0:T(8,128)(2,1)} %experts2.1.refs_4_), custom_call_target="tpu_custom_call" | custom-call | flops 35999997952 | bytes 1000 | tf_op jit(solution)/shard_map/experts3/pallas_call | solution.py:43
  205.2 3.6 %all-to-all-start.6 = ((bf16[8,24,3584]{2,1,0:T(8,128)(2,1)}), bf16[8,24,3584]{2,1,0:T(8,128)(2,1)S(1)}, u32[]{:S(2)}, u32[]{:S(2)}) async-start(bf16[8,24,3584]{2,1,0:T(8,128)(2,1)} %bitcast.28), calls=%async_computation.6 | async-start | bytes 2752512 | tf_op jit(solution)/shard_map/all_to_all | solution.py:256
  211.5 2.8 collective-permute-start.5
  214.3 13.3 %all-to-all-done.6 = bf16[8,24,3584]{2,1,0:T(8,128)(2,1)S(1)} async-done(((bf16[8,24,3584]{2,1,0:T(8,128)(2,1)}), bf16[8,24,3584]{2,1,0:T(8,128)(2,1)S(1)}, u32[]{:S(2)}, u32[]{:S(2)}) %all-to-all-start.6) | async-done | bytes 1376288 | tf_op jit(solution)/shard_map/all_to_all | solution.py:256
  227.6 4.3 %all-to-all-start.5 = ((bf16[8,24,3584]{2,1,0:T(8,128)(2,1)}), bf16[8,24,3584]{2,1,0:T(8,128)(2,1)}, u32[]{:S(2)}, u32[]{:S(2)}) async-start(bf16[8,24,3584]{2,1,0:T(8,128)(2,1)} %bitcast.21), calls=%async_computation.5 | async-start | bytes 2752512 | tf_op jit(solution)/shard_map/all_to_all | solution.py:256
  239.2 5.3 %collective-permute-start.8 = (bf16[128,3584]{1,0:T(8,128)(2,1)}, bf16[128,3584]{1,0:T(8,128)(2,1)}, u32[]{:S(2)}, u32[]{:S(2)}) collective-permute-start(bf16[128,3584]{1,0:T(8,128)(2,1)} %combine3.1.refs_2_.refs_0_), channel_id=1, source_target_pairs={{0,1},{3,2},{4,5},{7,6},{8,9},{11,10},{12,13},{15,14},{16,17},{19,... | collective-permute-start | bytes 2752520 | tf_op jit(solution)/shard_map/ppermute | solution.py:241
  244.5 6.3 %all-to-all-done.5 = bf16[8,24,3584]{2,1,0:T(8,128)(2,1)} async-done(((bf16[8,24,3584]{2,1,0:T(8,128)(2,1)}), bf16[8,24,3584]{2,1,0:T(8,128)(2,1)}, u32[]{:S(2)}, u32[]{:S(2)}) %all-to-all-start.5) | async-done | bytes 1376288 | tf_op jit(solution)/shard_map/all_to_all | solution.py:256
  250.8 2.7 combine1.1.refs_1_.refs_2_
  253.5 3.6 %all-to-all-start.7 = ((bf16[8,24,3584]{2,1,0:T(8,128)(2,1)}), bf16[8,24,3584]{2,1,0:T(8,128)(2,1)S(1)}, u32[]{:S(2)}, u32[]{:S(2)}) async-start(bf16[8,24,3584]{2,1,0:T(8,128)(2,1)} %bitcast.20), calls=%async_computation.7 | async-start | bytes 2752512 | tf_op jit(solution)/shard_map/all_to_all | solution.py:256
  260.5 4.1 %collective-permute-done.8.refs_1_ = bf16[128,3584]{1,0:T(8,128)(2,1)} collective-permute-done((bf16[128,3584]{1,0:T(8,128)(2,1)}, bf16[128,3584]{1,0:T(8,128)(2,1)}, u32[]{:S(2)}, u32[]{:S(2)}) %collective-permute-start.8) | collective-permute-done | bytes 917536 | tf_op jit(solution)/shard_map/ppermute | solution.py:241
  268.5 7.4 %all-to-all-done.7 = bf16[8,24,3584]{2,1,0:T(8,128)(2,1)S(1)} async-done(((bf16[8,24,3584]{2,1,0:T(8,128)(2,1)}), bf16[8,24,3584]{2,1,0:T(8,128)(2,1)S(1)}, u32[]{:S(2)}, u32[]{:S(2)}) %all-to-all-start.7) | async-done | bytes 1376288 | tf_op jit(solution)/shard_map/all_to_all | solution.py:256
  277.0 2.7 combine0.1.refs_0_
  279.8 21.6 %collective-permute-done.6.refs_1_ = bf16[128,3584]{1,0:T(8,128)(2,1)} collective-permute-done((bf16[128,3584]{1,0:T(8,128)(2,1)}, bf16[128,3584]{1,0:T(8,128)(2,1)}, u32[]{:S(2)}, u32[]{:S(2)}) %collective-permute-start.6) | collective-permute-done | bytes 917536 | tf_op jit(solution)/shard_map/ppermute | solution.py:241
  301.3 3.4 %add.7 = bf16[128,3584]{1,0:T(8,128)(2,1)} custom-call(bf16[128,3584]{1,0:T(8,128)(2,1)} %combine0.1.refs_0_, bf16[128,3584]{1,0:T(8,128)(2,1)} %collective-permute-done.6.refs_1_, bf16[128,3584]{1,0:T(8,128)(2,1)} %collective-permute-done.7.refs_2_, bf16[128,3584]{1,0:T(8,128)(2,1)} %collective-permute-done.9.refs_3_), custom_call_target="tpu_custom_call" | custom-call | flops 2000000 | bytes 1000 | tf_op jit(solution)/shard_map/add/pallas_call | solution.py:43
  (31 shorter events, 26.1 us)
Async XLA Ops:
  3.1 44.1 %collective-permute-start = (bf16[128,7296]{1,0:T(8,128)(2,1)}, bf16[128,7296]{1,0:T(8,128)(2,1)}, u32[]{:S(2)}, u32[]{:S(2)}) collective-permute-start(bf16[128,7296]{1,0:T(8,128)(2,1)} %route.1.refs_1_), channel_id=1, source_target_pairs={{0,1},{1,0},{2,3},{3,2},{4,5},{5,4},{6,7},{7,6},{8,9},{9,8},{10,11... | collective-permute-start | bytes 5603336 | tf_op jit(solution)/shard_map/ppermute | solution.py:241
  6.1 10.0 %collective-permute-start.1 = (bf16[128,7296]{1,0:T(8,128)(2,1)}, bf16[128,7296]{1,0:T(8,128)(2,1)S(1)}, u32[]{:S(2)}, u32[]{:S(2)}) collective-permute-start(bf16[128,7296]{1,0:T(8,128)(2,1)} %route.1.refs_1_), channel_id=1, source_target_pairs={{1,2},{2,1},{5,6},{6,5},{9,10},{10,9},{13,14},{14,13},{17,18},{18,... | collective-permute-start | bytes 5603336 | tf_op jit(solution)/shard_map/ppermute | solution.py:241
  11.6 41.6 %all-to-all-start = ((bf16[8,24,7168]{2,1,0:T(8,128)(2,1)}), bf16[8,24,7168]{2,1,0:T(8,128)(2,1)}, u32[]{:S(2)}, u32[]{:S(2)}) async-start(bf16[8,24,7168]{2,1,0:T(8,128)(2,1)} %bitcast.23), calls=%async_computation | async-start | bytes 5505024 | tf_op jit(solution)/shard_map/all_to_all | solution.py:256
  16.1 37.2 %copy-start.3 = (bf16[128,7296]{1,0:T(8,128)(2,1)}, bf16[128,7296]{1,0:T(8,128)(2,1)S(1)}, u32[]{:S(2)}) copy-start(bf16[128,7296]{1,0:T(8,128)(2,1)S(1)} %collective-permute-done.1.refs_1_) | copy-start | bytes 5603332
  16.1 77.0 %collective-permute-start.2 = (bf16[128,7296]{1,0:T(8,128)(2,1)S(1)}, bf16[128,7296]{1,0:T(8,128)(2,1)}, u32[]{:S(2)}, u32[]{:S(2)}) collective-permute-start(bf16[128,7296]{1,0:T(8,128)(2,1)S(1)} %collective-permute-done.1.refs_1_), channel_id=1, source_target_pairs={{1,0},{2,3},{5,4},{6,7},{9,8},{10,11},{13,12},{14,15},{17,16},{18,... | collective-permute-start | bytes 5603336 | tf_op jit(solution)/shard_map/ppermute | solution.py:241
  47.1 28.4 %collective-permute-start.3 = (bf16[128,7296]{1,0:T(8,128)(2,1)}, bf16[128,7296]{1,0:T(8,128)(2,1)}, u32[]{:S(2)}, u32[]{:S(2)}) collective-permute-start(bf16[128,7296]{1,0:T(8,128)(2,1)} %collective-permute-done.refs_1_), channel_id=1, source_target_pairs={{1,2},{2,1},{5,6},{6,5},{9,10},{10,9},{13,14},{14,13},{17,18},{18,... | collective-permute-start | bytes 5603336 | tf_op jit(solution)/shard_map/ppermute | solution.py:241
  53.3 44.5 %all-to-all-start.1 = ((bf16[8,24,7168]{2,1,0:T(8,128)(2,1)}), bf16[8,24,7168]{2,1,0:T(8,128)(2,1)}, u32[]{:S(2)}, u32[]{:S(2)}) async-start(bf16[8,24,7168]{2,1,0:T(8,128)(2,1)} %bitcast.22), calls=%async_computation.1 | async-start | bytes 5505024 | tf_op jit(solution)/shard_map/all_to_all | solution.py:256
  75.5 63.3 %collective-permute-start.4 = (bf16[128,7296]{1,0:T(8,128)(2,1)}, bf16[128,7296]{1,0:T(8,128)(2,1)}, u32[]{:S(2)}, u32[]{:S(2)}) collective-permute-start(bf16[128,7296]{1,0:T(8,128)(2,1)} %collective-permute-done.3.refs_1_), channel_id=1, source_target_pairs={{1,0},{2,3},{5,4},{6,7},{9,8},{10,11},{13,12},{14,15},{17,16},{18,... | collective-permute-start | bytes 5603336 | tf_op jit(solution)/shard_map/ppermute | solution.py:241
  97.8 45.8 %all-to-all-start.2 = ((bf16[8,24,7168]{2,1,0:T(8,128)(2,1)}), bf16[8,24,7168]{2,1,0:T(8,128)(2,1)}, u32[]{:S(2)}, u32[]{:S(2)}) async-start(bf16[8,24,7168]{2,1,0:T(8,128)(2,1)} %bitcast.24), calls=%async_computation.2 | async-start | bytes 5505024 | tf_op jit(solution)/shard_map/all_to_all | solution.py:256
  143.5 38.1 %all-to-all-start.4 = ((bf16[8,24,7168]{2,1,0:T(8,128)(2,1)}), bf16[8,24,7168]{2,1,0:T(8,128)(2,1)}, u32[]{:S(2)}, u32[]{:S(2)}) async-start(bf16[8,24,7168]{2,1,0:T(8,128)(2,1)} %bitcast.25), calls=%async_computation.4 | async-start | bytes 5505024 | tf_op jit(solution)/shard_map/all_to_all | solution.py:256
  181.7 22.4 %all-to-all-start.3 = ((bf16[8,24,3584]{2,1,0:T(8,128)(2,1)}), bf16[8,24,3584]{2,1,0:T(8,128)(2,1)S(1)}, u32[]{:S(2)}, u32[]{:S(2)}) async-start(bf16[8,24,3584]{2,1,0:T(8,128)(2,1)} %bitcast.30), calls=%async_computation.3 | async-start | bytes 2752512 | tf_op jit(solution)/shard_map/all_to_all | solution.py:256
  204.1 1.1 copy-start.2
  205.2 22.4 %all-to-all-start.6 = ((bf16[8,24,3584]{2,1,0:T(8,128)(2,1)}), bf16[8,24,3584]{2,1,0:T(8,128)(2,1)S(1)}, u32[]{:S(2)}, u32[]{:S(2)}) async-start(bf16[8,24,3584]{2,1,0:T(8,128)(2,1)} %bitcast.28), calls=%async_computation.6 | async-start | bytes 2752512 | tf_op jit(solution)/shard_map/all_to_all | solution.py:256
  211.5 22.4 %collective-permute-start.5 = (bf16[128,3584]{1,0:T(8,128)(2,1)}, bf16[128,3584]{1,0:T(8,128)(2,1)}, u32[]{:S(2)}, u32[]{:S(2)}) collective-permute-start(bf16[128,3584]{1,0:T(8,128)(2,1)} %combine2.1.refs_1_.refs_0_.refs_2_), channel_id=1, source_target_pairs={{0,1},{3,2},{4,5},{7,6},{8,9},{11,10},{12,13},{15,14},{16,17},{19,... | collective-permute-start | bytes 2752520 | tf_op jit(solution)/shard_map/ppermute | solution.py:241
  227.6 8.8 %copy-start = (bf16[8,24,3584]{2,1,0:T(8,128)(2,1)}, bf16[8,24,3584]{2,1,0:T(8,128)(2,1)S(1)}, u32[]{:S(2)}) copy-start(bf16[8,24,3584]{2,1,0:T(8,128)(2,1)S(1)} %all-to-all-done.6) | copy-start | bytes 4128772
  227.6 23.2 %all-to-all-start.5 = ((bf16[8,24,3584]{2,1,0:T(8,128)(2,1)}), bf16[8,24,3584]{2,1,0:T(8,128)(2,1)}, u32[]{:S(2)}, u32[]{:S(2)}) async-start(bf16[8,24,3584]{2,1,0:T(8,128)(2,1)} %bitcast.21), calls=%async_computation.5 | async-start | bytes 2752512 | tf_op jit(solution)/shard_map/all_to_all | solution.py:256
  239.2 25.5 %collective-permute-start.8 = (bf16[128,3584]{1,0:T(8,128)(2,1)}, bf16[128,3584]{1,0:T(8,128)(2,1)}, u32[]{:S(2)}, u32[]{:S(2)}) collective-permute-start(bf16[128,3584]{1,0:T(8,128)(2,1)} %combine3.1.refs_2_.refs_0_), channel_id=1, source_target_pairs={{0,1},{3,2},{4,5},{7,6},{8,9},{11,10},{12,13},{15,14},{16,17},{19,... | collective-permute-start | bytes 2752520 | tf_op jit(solution)/shard_map/ppermute | solution.py:241
  253.5 22.4 %all-to-all-start.7 = ((bf16[8,24,3584]{2,1,0:T(8,128)(2,1)}), bf16[8,24,3584]{2,1,0:T(8,128)(2,1)S(1)}, u32[]{:S(2)}, u32[]{:S(2)}) async-start(bf16[8,24,3584]{2,1,0:T(8,128)(2,1)} %bitcast.20), calls=%async_computation.7 | async-start | bytes 2752512 | tf_op jit(solution)/shard_map/all_to_all | solution.py:256
  257.1 22.7 %collective-permute-start.7 = (bf16[128,3584]{1,0:T(8,128)(2,1)}, bf16[128,3584]{1,0:T(8,128)(2,1)}, u32[]{:S(2)}, u32[]{:S(2)}) collective-permute-start(bf16[128,3584]{1,0:T(8,128)(2,1)} %add.5.refs_3_), channel_id=1, source_target_pairs={{1,2},{2,1},{5,6},{6,5},{9,10},{10,9},{13,14},{14,13},{17,18},{18,... | collective-permute-start | bytes 2752520 | tf_op jit(solution)/shard_map/ppermute | solution.py:241
  258.7 42.6 %collective-permute-start.6 = (bf16[128,3584]{1,0:T(8,128)(2,1)}, bf16[128,3584]{1,0:T(8,128)(2,1)}, u32[]{:S(2)}, u32[]{:S(2)}) collective-permute-start(bf16[128,3584]{1,0:T(8,128)(2,1)} %combine1.1.refs_1_.refs_2_), channel_id=1, source_target_pairs={{0,1},{1,0},{2,3},{3,2},{4,5},{5,4},{6,7},{7,6},{8,9},{9,8},{10,11... | collective-permute-start | bytes 2752520 | tf_op jit(solution)/shard_map/ppermute | solution.py:241
  267.2 34.1 %collective-permute-start.9 = (bf16[128,3584]{1,0:T(8,128)(2,1)}, bf16[128,3584]{1,0:T(8,128)(2,1)}, u32[]{:S(2)}, u32[]{:S(2)}) collective-permute-start(bf16[128,3584]{1,0:T(8,128)(2,1)} %add.6), channel_id=1, source_target_pairs={{1,3},{2,0},{5,7},{6,4},{9,11},{10,8},{13,15},{14,12},{17,19},{18,... | collective-permute-start | bytes 2752520 | tf_op jit(solution)/shard_map/ppermute | solution.py:241
  275.9 1.1 copy-start.1
